TPU v7x, 32 devices: a whole 2x2x4 slice. The times are simulated.
32 devices in a mesh: dp: 4 (over y, core), tensor: 8 (over z, x).
Axes of the slice: x: 2, y: 2, z: 4, core: 2. Of those that a mesh axis runs over, the one named last changes fastest.
Arguments:
- features: bfloat16 [512, 4096], P('dp'), may hold values from -6 to 6
- enc_in: bfloat16 [4096, 2048], P(None, 'tensor'), may hold values from -0.09375 to 0.09375
- enc_out: bfloat16 [2048, 8192], P('tensor'), may hold values from -0.125 to 0.125
- noise: bfloat16 [512, 4096], P('dp', 'tensor'), may hold values from -6 to 6
- in_weight: bfloat16 [4096, 16384], P('dp', 'tensor'), may hold values from -0.09375 to 0.09375
- out_weight: bfloat16 [4096, 16384], P('dp', 'tensor'), may hold values from -0.046875 to 0.046875
- probes: bfloat16 [2, 512, 4096], P(None, 'dp'), may hold values from -6 to 6
Outputs:
- flowed: float32 [512, 4096], P('dp', 'tensor')
- logdet: float32 [512], P('dp')
All inputs are finite; a program needn't handle non-finite values.
Results may differ from a plain program's by a relative error of at most 0.017.
Values may be sent and summed in bfloat16 or wider, within the bound.
A program may use at most 128 MiB of HBM per device.

v0:
```python
import jax
import jax.numpy as jnp
from jax import lax
from jax.sharding import PartitionSpec as P

L = 4096
PROBES = 2
TERMS = 3


def collect(partial_value):
    return lax.psum(partial_value.astype(jnp.bfloat16), "tensor")


def series(start, w_in, w_out, slope):
    start32 = start.astype(jnp.float32)
    current = start
    running = jnp.zeros((start.shape[1],), jnp.float32)
    for term_idx in range(TERMS):
        pulled = jnp.einsum("pbl,lh->pbh", current, w_out, preferred_element_type=jnp.float32)
        scaled = (pulled * slope[None]).astype(jnp.bfloat16)
        partial_value = jnp.einsum("pbh,lh->pbl", scaled, w_in, preferred_element_type=jnp.float32)
        current = collect(partial_value)
        coeff = (-1.0) ** term_idx / (term_idx + 1)
        running = running + coeff * jnp.sum(start32 * current.astype(jnp.float32), axis=(0, 2))
    return running


def local(features, enc_in, enc_out, noise, in_weight, out_weight, probes):
    hidden = jax.nn.silu(jnp.dot(features, enc_in, preferred_element_type=jnp.float32)).astype(
        jnp.bfloat16
    )
    partial_stats = jnp.dot(hidden, enc_out, preferred_element_type=jnp.float32)
    batch_rows = partial_stats.shape[0]
    moments = lax.psum_scatter(
        partial_stats.reshape(batch_rows, 2, L), "tensor", scatter_dimension=2, tiled=True
    )
    u_slice = (moments[:, 0] + jax.nn.softplus(moments[:, 1]) * noise.astype(jnp.float32)).astype(
        jnp.bfloat16
    )
    u_full = lax.all_gather(u_slice, "tensor", axis=1, tiled=True)
    w_in, w_out = (
        lax.all_gather(in_weight, "dp", axis=0, tiled=True),
        lax.all_gather(out_weight, "dp", axis=0, tiled=True),
    )
    pre_act = jnp.dot(u_full, w_in, preferred_element_type=jnp.float32)
    tanh_val = jnp.tanh(pre_act)
    squash = tanh_val.astype(jnp.bfloat16)
    slope = 1.0 - tanh_val * tanh_val
    branch_part = jnp.einsum("bh,lh->bl", squash, w_out, preferred_element_type=jnp.float32)
    flowed = u_slice.astype(jnp.float32) + lax.psum_scatter(
        branch_part.astype(jnp.bfloat16), "tensor", scatter_dimension=1, tiled=True
    ).astype(jnp.float32)
    running = series(probes, w_in, w_out, slope)
    logdet = running / PROBES
    return (flowed, logdet)


def solution(mesh):
    in_specs = (
        P("dp", None),
        P(None, "tensor"),
        P("tensor", None),
        P("dp", "tensor"),
        P("dp", "tensor"),
        P("dp", "tensor"),
        P(None, "dp", None),
    )
    out_specs = (P("dp", "tensor"), P("dp"))
    return jax.shard_map(local, mesh=mesh, in_specs=in_specs, out_specs=out_specs, check_vma=False)
```

profile of v0, /device:TPU:6, one launch (start us, length us, event | category | flops | bytes accessed | tf_op | source)
XLA Modules:
  0.0 790.9 jit_solution(8963951383213202102)
XLA Ops:
  7.2 0.0 copy-start
  7.2 0.0 reduce-scatter.3.cloned.1.call-start
  7.2 1.5 copy-done
  8.8 6.1 fusion.46
  14.9 4.6 copy.12
  19.5 0.0 copy-start.5
  19.5 0.0 reduce-scatter.3.cloned.1.call-update
  19.5 0.0 all-gather.4.cloned.1.call-start
  19.5 89.8 %reduce-scatter.3.cloned.1.call-done = f32[128,2,512]{2,0,1:T(8,128)} async-done(((f32[128,2,4096]{2,0,1:T(8,128)}), f32[128,2,512]{2,0,1:T(8,128)}) %reduce-scatter.3.cloned.1.call-update) | async-done | bytes 524304 | tf_op jit(solution)/shard_map/reduce_scatter | solution.py:35
  109.3 0.0 copy-done.5
  109.3 1.9 fusion.45
  111.2 0.0 all-gather.4.cloned.1.call-update
  111.2 0.0 all-gather.6.cloned.1.call-start
  111.3 0.7 all-gather.6.cloned.1.call-update
  111.9 0.0 all-gather.8.cloned.1.call-start
  112.0 0.5 all-gather.8.cloned.1.call-update
  112.5 0.0 copy-start.2
  112.5 0.0 all-reduce.4.cloned.1.call-start
  112.6 38.6 %all-gather.4.cloned.1.call-done = bf16[128,4096]{1,0:T(8,128)(2,1)} async-done(((bf16[128,512]{1,0:T(8,128)(2,1)}), bf16[128,4096]{1,0:T(8,128)(2,1)}) %all-gather.4.cloned.1.call-update) | async-done | bytes 1048592 | tf_op jit(solution)/shard_map/all_gather | solution.py:41
  151.2 105.8 %all-gather.6.cloned.1.call-done = bf16[4096,2048]{1,0:T(8,128)(2,1)} async-done(((bf16[1024,2048]{1,0:T(8,128)(2,1)}), bf16[4096,2048]{1,0:T(8,128)(2,1)}) %all-gather.6.cloned.1.call-update) | async-done | bytes 16777232 | tf_op jit(solution)/shard_map/all_gather | solution.py:43
  257.0 9.5 %multiply_subtract_fusion = (f32[128,2048]{1,0:T(8,128)}, bf16[128,2048]{1,0:T(8,128)(2,1)S(1)}) fusion(bf16[128,4096]{1,0:T(8,128)(2,1)} %all-gather.4.cloned.1.call-done, bf16[4096,2048]{1,0:T(8,128)(2,1)} %all-gather.6.cloned.1.call-done), kind=kOutput, calls=%fused_computation.30 | convolution fusion | flops 2148270080 | bytes 19398656 | tf_op jit(solution)/shard_map/dot_general | solution.py:46
  266.5 98.0 %all-gather.8.cloned.1.call-done = bf16[4096,2048]{1,0:T(8,128)(2,1)} async-done(((bf16[1024,2048]{1,0:T(8,128)(2,1)}), bf16[4096,2048]{1,0:T(8,128)(2,1)}) %all-gather.8.cloned.1.call-update) | async-done | bytes 16777232 | tf_op jit(solution)/shard_map/all_gather | solution.py:44
  364.5 0.0 copy-done.2
  364.5 17.0 %fusion.12 = bf16[2,128,4096]{2,1,0:T(8,128)(2,1)} fusion(bf16[4096,2048]{1,0:T(8,128)(2,1)} %all-gather.6.cloned.1.call-done, bf16[2,128,4096]{2,1,0:T(8,128)(2,1)S(1)} %copy-done.2, bf16[4096,2048]{1,0:T(8,128)(2,1)} %all-gather.8.cloned.1.call-done, f32[128,2048]{1,0:T(8,128)} %get-tuple-element.5), kind=kOutput, calls=%fused_computation.15 | convolution fusion | flops 8592031744 | bytes 38797312 | tf_op jit(solution)/shard_map/pbh,lh->pbl/dot_general | solution.py:22
  381.5 0.0 all-reduce.4.cloned.1.call-update
  381.5 0.2 all-reduce.6.cloned.1.call-start
  381.8 102.6 %all-reduce.4.cloned.1.call-done = bf16[2,128,4096]{2,1,0:T(8,128)(2,1)} async-done(((bf16[2,128,4096]{2,1,0:T(8,128)(2,1)}), bf16[2,128,4096]{2,1,0:T(8,128)(2,1)}) %all-reduce.4.cloned.1.call-update) | async-done | bytes 2097168 | tf_op jit(solution)/shard_map/psum | solution.py:12
  484.4 20.6 %fusion.15 = bf16[2,128,4096]{2,1,0:T(8,128)(2,1)} fusion(bf16[4096,2048]{1,0:T(8,128)(2,1)} %all-gather.6.cloned.1.call-done, bf16[2,128,4096]{2,1,0:T(8,128)(2,1)} %all-reduce.4.cloned.1.call-done, bf16[4096,2048]{1,0:T(8,128)(2,1)} %all-gather.8.cloned.1.call-done, f32[128,2048]{1,0:T(8,128)} %get-tuple-element.5), kind=kOutput, calls=%fused_computation.16 | convolution fusion | flops 8592031744 | bytes 38797312 | tf_op jit(solution)/shard_map/pbh,lh->pbl/dot_general | solution.py:22
  505.0 0.0 all-reduce.6.cloned.1.call-update
  505.0 0.0 reduce-scatter.5.cloned.1.call-start
  505.1 0.0 copy-start.4
  505.1 12.7 %convolution_convert_fusion = bf16[128,4096]{1,0:T(8,128)(2,1)} fusion(bf16[4096,2048]{1,0:T(8,128)(2,1)} %all-gather.8.cloned.1.call-done, bf16[128,2048]{1,0:T(8,128)(2,1)S(1)} %get-tuple-element.6), kind=kOutput, calls=%fused_computation.18 | convolution fusion | flops 2148007936 | bytes 18350080 | tf_op jit(solution)/shard_map/bh,lh->bl/dot_general | solution.py:50
  517.8 0.0 reduce-scatter.5.cloned.1.call-update
  517.8 0.0 copy-start.3
  517.8 0.3 all-reduce.8.cloned.1.call-start
  518.1 88.6 %all-reduce.6.cloned.1.call-done = bf16[2,128,4096]{2,1,0:T(8,128)(2,1)} async-done(((bf16[2,128,4096]{2,1,0:T(8,128)(2,1)}), bf16[2,128,4096]{2,1,0:T(8,128)(2,1)}) %all-reduce.6.cloned.1.call-update) | async-done | bytes 2097168 | tf_op jit(solution)/shard_map/psum | solution.py:12
  606.7 0.0 copy-done.4
  606.7 17.2 %fusion.18 = bf16[2,128,4096]{2,1,0:T(8,128)(2,1)} fusion(bf16[4096,2048]{1,0:T(8,128)(2,1)} %all-gather.6.cloned.1.call-done, bf16[2,128,4096]{2,1,0:T(8,128)(2,1)} %all-reduce.6.cloned.1.call-done, bf16[4096,2048]{1,0:T(8,128)(2,1)} %all-gather.8.cloned.1.call-done, f32[128,2048]{1,0:T(8,128)S(1)} %copy-done.4), kind=kOutput, calls=%fused_computation.17 | convolution fusion | flops 8592031744 | bytes 38797312 | tf_op jit(solution)/shard_map/pbh,lh->pbl/dot_general | solution.py:22
  623.9 0.0 all-reduce.8.cloned.1.call-update
  623.9 49.9 %reduce-scatter.5.cloned.1.call-done = bf16[128,512]{1,0:T(8,128)(2,1)} async-done(((bf16[128,4096]{1,0:T(8,128)(2,1)}), bf16[128,512]{1,0:T(8,128)(2,1)}) %reduce-scatter.5.cloned.1.call-update) | async-done | bytes 131088 | tf_op jit(solution)/shard_map/reduce_scatter | solution.py:51
  673.8 0.0 copy-done.3
  673.8 0.0 copy-start.1
  673.8 1.8 convert_add_fusion
  675.5 103.0 %all-reduce.8.cloned.1.call-done = bf16[2,128,4096]{2,1,0:T(8,128)(2,1)} async-done(((bf16[2,128,4096]{2,1,0:T(8,128)(2,1)}), bf16[2,128,4096]{2,1,0:T(8,128)(2,1)}) %all-reduce.8.cloned.1.call-update) | async-done | bytes 2097168 | tf_op jit(solution)/shard_map/psum | solution.py:12
  778.5 5.0 fusion.22
  783.5 0.5 add_multiply_fusion
  784.0 0.0 copy-done.1
Async XLA Ops:
  7.2 1.6 copy-start
  7.2 102.1 %reduce-scatter.3.cloned.1.call-start = ((), (), s32[]{:S(2)}) async-start(), calls=%async_computation.2 | async-start | bytes 4718592 | tf_op jit(solution)/shard_map/reduce_scatter | solution.py:35
  19.5 89.9 %copy-start.5 = (bf16[128,512]{1,0:T(8,128)(2,1)S(1)}, bf16[128,512]{1,0:T(8,128)(2,1)}, u32[]{:S(2)}) copy-start(bf16[128,512]{1,0:T(8,128)(2,1)} %param.10) | copy-start | bytes 393220
  19.5 131.7 %all-gather.4.cloned.1.call-start = ((), (), s32[]{:S(2)}) async-start(), calls=%async_computation.3 | async-start | bytes 1179648 | tf_op jit(solution)/shard_map/all_gather | solution.py:41
  111.2 145.8 %all-gather.6.cloned.1.call-start = ((), (), s32[]{:S(2)}) async-start(), calls=%async_computation.4 | async-start | bytes 20971520 | tf_op jit(solution)/shard_map/all_gather | solution.py:43
  111.9 252.5 %all-gather.8.cloned.1.call-start = ((), (), s32[]{:S(2)}) async-start(), calls=%async_computation.5 | async-start | bytes 20971520 | tf_op jit(solution)/shard_map/all_gather | solution.py:44
  112.5 252.0 %copy-start.2 = (bf16[2,128,4096]{2,1,0:T(8,128)(2,1)S(1)}, bf16[2,128,4096]{2,1,0:T(8,128)(2,1)}, u32[]{:S(2)}) copy-start(bf16[2,128,4096]{2,1,0:T(8,128)(2,1)} %param.13) | copy-start | bytes 6291460
  112.5 371.8 %all-reduce.4.cloned.1.call-start = ((), (), s32[]{:S(2)}) async-start(), calls=%async_computation.7 | async-start | bytes 4194304 | tf_op jit(solution)/shard_map/psum | solution.py:12
  381.5 225.1 %all-reduce.6.cloned.1.call-start = ((), (), s32[]{:S(2)}) async-start(), calls=%async_computation.8 | async-start | bytes 4194304 | tf_op jit(solution)/shard_map/psum | solution.py:12
  505.0 168.7 %reduce-scatter.5.cloned.1.call-start = ((), (), s32[]{:S(2)}) async-start(), calls=%async_computation.6 | async-start | bytes 1179648 | tf_op jit(solution)/shard_map/reduce_scatter | solution.py:51
  505.1 101.6 %copy-start.4 = (f32[128,2048]{1,0:T(8,128)S(1)}, f32[128,2048]{1,0:T(8,128)}, u32[]{:S(2)}) copy-start(f32[128,2048]{1,0:T(8,128)} %get-tuple-element.5) | copy-start | bytes 3145732
  517.8 156.0 %copy-start.3 = (bf16[128,512]{1,0:T(8,128)(2,1)S(1)}, bf16[128,512]{1,0:T(8,128)(2,1)}, u32[]{:S(2)}) copy-start(bf16[128,512]{1,0:T(8,128)(2,1)} %fusion.45) | copy-start | bytes 393220
  517.8 260.7 %all-reduce.8.cloned.1.call-start = ((), (), s32[]{:S(2)}) async-start(), calls=%async_computation.9 | async-start | bytes 4194304 | tf_op jit(solution)/shard_map/psum | solution.py:12
  673.8 110.3 %copy-start.1 = (bf16[4096,256]{1,0:T(8,128)(2,1)S(1)}, bf16[4096,256]{1,0:T(8,128)(2,1)}, u32[]{:S(2)}) copy-start(bf16[4096,256]{1,0:T(8,128)(2,1)} %param.8) | copy-start | bytes 6291460
Sparse Core Ops, SparseCore 0:
  19.6 89.6 reduce-scatter.2
  112.1 39.0 all-gather.3
  152.8 104.1 all-gather.5
  258.5 105.9 all-gather.7
  381.7 102.6 all-reduce.3
  505.1 101.4 all-reduce.5
  610.4 63.2 reduce-scatter.4
  677.4 101.1 all-reduce.7
where the time goes:
time: 793 us; the launch traced here: 791 us
  waiting for transfers between devices  678 us (85%)
  matrix products  83.2 us (10%)
  between operations  14.2 us (2%)
  other arithmetic  9.12 us (1%)
    psum x3, waiting for transfers between devices, collect(): return lax.psum(partial_value.astype(jnp.bfloat16), 'tensor')  294 us
    all_gather x1, waiting for transfers between devices, local(): lax.all_gather(in_weight, 'dp', axis=0, tiled=True)  106 us
    all_gather x1, waiting for transfers between devices, local(): lax.all_gather(out_weight, 'dp', axis=0, tiled=True)  98 us
    reduce_scatter x1, waiting for transfers between devices, local(): lax.psum_scatter(partial_stats.reshape(batch_rows, 2, L), 'tensor', scatt...  89.8 us
    dot_general x3, matrix products, series(): jnp.einsum('pbh,lh->pbl', scaled, w_in, preferred_element_type=jnp.float32)  54.9 us
    reduce_scatter x1, waiting for transfers between devices, local(): lax.psum_scatter(branch_part.astype(jnp.bfloat16), 'tensor', scatter_dime...  49.9 us
    all_gather x1, waiting for transfers between devices, local(): u_full = lax.all_gather(u_slice, 'tensor', axis=1, tiled=True)  38.6 us
  transfers between devices with their start and end apart: 8, of which 8 were waited for; matrix products, arithmetic and copies ran while one was open for 5% of the time, Pallas kernels for 0%

commit v1 on v0

v1 whole, which is shorter than its diff:
```python
import jax
import jax.numpy as jnp
from jax import lax
from jax.sharding import PartitionSpec as P


def dot(a, b):
    return jnp.dot(a, b, preferred_element_type=jnp.float32)


def dot_t(a, b):
    return lax.dot_general(a, b, (((1,), (1,)), ((), ())), preferred_element_type=jnp.float32)


def gather_blocks(shard, n):
    half = n // 2
    swap = [(d, d ^ 1) for d in range(n)]
    blocks = []
    for k in range(half):
        own = shard
        if k:
            own = lax.ppermute(
                shard, "dp", [(((y + k) % half) * 2 + c, y * 2 + c) for y in range(half) for c in range(2)]
            )
        blocks += [own, lax.ppermute(own, "dp", swap)]
    return blocks


def owners(n):
    me = lax.axis_index("dp")
    core = lax.rem(me, 2)
    y = lax.div(me, 2)
    half = n // 2
    out = []
    for k in range(half):
        yk = lax.rem(y + k, half)
        out += [yk * 2 + core, yk * 2 + 1 - core]
    return out


def make_local(n, t):
    def local(features, enc_in, enc_out, noise, in_weight, out_weight, probes):
        rows = features.shape[0]
        depth = in_weight.shape[0]
        latents = depth * n
        n_probes = probes.shape[0]
        w_in = gather_blocks(in_weight, n)
        w_out = gather_blocks(out_weight, n)
        own = owners(n)

        def cols(x):
            return [lax.dynamic_slice_in_dim(x, o * depth, depth, 1) for o in own]

        hidden = jax.nn.silu(dot(features, enc_in)).astype(jnp.bfloat16)
        partial_stats = dot(hidden, enc_out)
        moments = lax.psum_scatter(
            partial_stats.reshape(rows, 2, latents), "tensor", scatter_dimension=2, tiled=True
        )
        u_slice = (
            moments[:, 0] + jax.nn.softplus(moments[:, 1]) * noise.astype(jnp.float32)
        ).astype(jnp.bfloat16)
        u_full = lax.all_gather(u_slice, "tensor", axis=1, tiled=True)

        start = cols(probes.reshape(n_probes * rows, latents))
        q = sum(dot(a, w) for a, w in zip(start, w_in))
        pre_act = sum(dot(a, w) for a, w in zip(cols(u_full), w_in))
        tanh_val = jnp.tanh(pre_act)
        squash = tanh_val.astype(jnp.bfloat16)
        slope = jnp.tile(1.0 - tanh_val * tanh_val, (n_probes, 1))
        sq = q * slope
        sq16 = sq.astype(jnp.bfloat16)
        r = sum(dot(a, w) for a, w in zip(start, w_out))
        sr16 = (r * slope).astype(jnp.bfloat16)
        first = jnp.sum(sq * r, axis=1)

        both = [
            jnp.concatenate([dot_t(sr16, wi), dot_t(sq16, wo)], 0).astype(jnp.bfloat16)
            for wi, wo in zip(w_in, w_out)
        ]
        both = lax.psum(jnp.concatenate(both, 1), "tensor")
        w1, y1 = both[: n_probes * rows], both[n_probes * rows :]
        second = jnp.sum(w1.astype(jnp.float32) * y1.astype(jnp.float32), axis=1) / t
        left = sum(dot(y1[:, i * depth : (i + 1) * depth], w) for i, w in enumerate(w_in))
        right = sum(dot(w1[:, i * depth : (i + 1) * depth], w) for i, w in enumerate(w_out))
        third = jnp.sum(left * slope * right, axis=1)
        logdet = lax.psum(
            jnp.sum((first - second / 2 + third / 3).reshape(n_probes, rows), 0), "tensor"
        ) / n_probes

        branch = jnp.zeros((rows, latents), jnp.bfloat16)
        for o, w in zip(own, w_out):
            branch = lax.dynamic_update_slice_in_dim(
                branch, dot_t(squash, w).astype(jnp.bfloat16), o * depth, 1
            )
        flowed = u_slice.astype(jnp.float32) + lax.psum_scatter(
            branch, "tensor", scatter_dimension=1, tiled=True
        ).astype(jnp.float32)
        return flowed, logdet

    return local


def solution(mesh):
    in_specs = (
        P("dp", None),
        P(None, "tensor"),
        P("tensor", None),
        P("dp", "tensor"),
        P("dp", "tensor"),
        P("dp", "tensor"),
        P(None, "dp", None),
    )
    out_specs = (P("dp", "tensor"), P("dp"))
    local = make_local(mesh.shape["dp"], mesh.shape["tensor"])
    return jax.shard_map(local, mesh=mesh, in_specs=in_specs, out_specs=out_specs, check_vma=False)
```

time: 793 us -> 558 us (0.70)
  waiting for transfers between devices: 678 us -> 350 us
  matrix products: 83.2 us -> 119 us
  other arithmetic: 9.12 us -> 38.2 us
  blocking collectives: 0 us -> 17.7 us
    all_gather x2 -> x0, waiting for transfers between devices: 204 us -> none  [the longest x1 106 us: local(): lax.all_gather(in_weight, 'dp', axis=0, tiled=True)]
    ppermute x0 -> x6, waiting for transfers between devices: none -> 172 us  [the longest x2 172 us: gather_blocks(): lax.ppermute(shard, 'dp', [((y + k) % half * 2 + c, y * 2 + c) for y in r...]
    reduce_scatter x2, waiting for transfers between devices: 140 us -> 0.02 us  [the longest x1 0.02 us: local(): lax.psum_scatter(branch, 'tensor', scatter_dimension=1, tiled=True)]
    psum x3 -> x1, waiting for transfers between devices: 294 us -> 155 us  [local(): both = lax.psum(jnp.concatenate(both, 1), 'tensor')]
    dot_general x6 -> x33, matrix products: 83.2 us -> 119 us  [the longest x21 78.7 us: dot(): return jnp.dot(a, b, preferred_element_type=jnp.float32)]
    concatenate x0 -> x1, other arithmetic: none -> 31.2 us  [local(): both = lax.psum(jnp.concatenate(both, 1), 'tensor')]
    psum x0 -> x1, blocking collectives: none -> 17.7 us  [local(): lax.psum(jnp.sum((first - second / 2 + third / 3).reshape(n_probes, rows)...]
    all_gather x1, waiting for transfers between devices: 38.6 us -> 22.6 us  [local(): u_full = lax.all_gather(u_slice, 'tensor', axis=1, tiled=True)]
  transfers between devices with their start and end apart: 8 -> 10, of which waited for: 8 -> 4; matrix products, arithmetic and copies ran while one was open for 5% -> 21% of each run, Pallas kernels for 0% -> 0%
where the time goes in v1:
time: 558 us; the launch traced here: 550 us
  waiting for transfers between devices  350 us (63%)
  matrix products  119 us (21%)
  other arithmetic  38.2 us (7%)
  blocking collectives  17.7 us (3%)
  between operations  14.4 us (3%)
  local copies, waits for them, and re-layouts  7.94 us (1%)
    ppermute x2, waiting for transfers between devices, gather_blocks(): lax.ppermute(shard, 'dp', [((y + k) % half * 2 + c, y * 2 + c) for y in r...  172 us
    psum x1, waiting for transfers between devices, local(): both = lax.psum(jnp.concatenate(both, 1), 'tensor')  155 us
    dot_general x21, matrix products, dot(): return jnp.dot(a, b, preferred_element_type=jnp.float32)  78.7 us
    dot_general x12, matrix products, dot_t(): lax.dot_general(a, b, (((1,), (1,)), ((), ())), preferred_element_type=jn...  39.8 us
    concatenate x1, other arithmetic, local(): both = lax.psum(jnp.concatenate(both, 1), 'tensor')  31.2 us
    all_gather x1, waiting for transfers between devices, local(): u_full = lax.all_gather(u_slice, 'tensor', axis=1, tiled=True)  22.6 us
    psum x1, blocking collectives, local(): lax.psum(jnp.sum((first - second / 2 + third / 3).reshape(n_probes, rows)...  17.7 us
  transfers between devices with their start and end apart: 10, of which 4 were waited for; matrix products, arithmetic and copies ran while one was open for 21% of the time, Pallas kernels for 0%

profile of v1, /device:TPU:6, one launch (start us, length us, event | category | flops | bytes accessed | tf_op | source)
XLA Modules:
  0.0 549.9 jit_solution(10289635483011457413)
XLA Ops:
  7.2 0.0 copy-start
  7.2 0.0 reduce-scatter.3.cloned.1.call-start
  7.2 6.9 %fusion.36 = f32[128,8192]{1,0:T(8,128)} fusion(bf16[256,8192]{1,0:T(8,128)(2,1)} %param.9, bf16[128,4096]{1,0:T(8,128)(2,1)} %param.7, bf16[4096,256]{1,0:T(8,128)(2,1)} %param.8), kind=kOutput, calls=%fused_computation.76 | convolution fusion | flops 805470208 | bytes 11534336 | tf_op jit(solution)/shard_map/dot_general | solution.py:8
  14.1 4.6 copy.13
  18.7 0.0 reduce-scatter.3.cloned.1.call-update
  18.7 0.0 all-gather.2.cloned.1.call-start
  18.8 0.6 collective-permute-start.1
  19.4 1.5 collective-permute-start.4
  20.9 0.5 collective-permute-start.3
  21.4 91.2 %collective-permute-done.1 = bf16[1024,2048]{1,0:T(8,128)(2,1)} collective-permute-done((bf16[1024,2048]{1,0:T(8,128)(2,1)}, bf16[1024,2048]{1,0:T(8,128)(2,1)}, u32[]{:S(2)}, u32[]{:S(2)}) %collective-permute-start.1) | collective-permute-done | bytes 4194336 | tf_op jit(solution)/shard_map/ppermute | solution.py:22
  112.6 4.9 fusion.24
  117.6 2.6 fusion.26
  120.1 81.2 %collective-permute-done.4 = bf16[1024,2048]{1,0:T(8,128)(2,1)} collective-permute-done((bf16[1024,2048]{1,0:T(8,128)(2,1)}, bf16[1024,2048]{1,0:T(8,128)(2,1)}, u32[]{:S(2)}, u32[]{:S(2)}) %collective-permute-start.4) | collective-permute-done | bytes 4194336 | tf_op jit(solution)/shard_map/ppermute | solution.py:22
  201.4 1.9 fusion.30
  203.2 0.0 all-gather.2.cloned.1.call-update
  203.2 0.6 reduce-scatter.5.cloned.1.call-start
  203.8 4.1 convolution_add_fusion.11
  208.0 5.0 convolution_add_fusion.10
  213.0 3.5 convolution_add_fusion.8
  216.5 4.9 convolution_add_fusion.7
  221.4 22.6 %all-gather.2.cloned.1.call-done = bf16[128,4096]{1,0:T(8,128)(2,1)} async-done(((bf16[128,512]{1,0:T(8,128)(2,1)}), bf16[128,4096]{1,0:T(8,128)(2,1)}) %all-gather.2.cloned.1.call-update) | async-done | bytes 1048592 | tf_op jit(solution)/shard_map/all_gather | solution.py:62
  244.0 3.1 fusion.34
  247.1 3.0 convolution_add_fusion.14
  250.0 3.0 convolution_add_fusion.13
  253.0 3.2 multiply_subtract_fusion
  256.2 1.1 broadcast_in_dim.3
  257.3 2.2 fusion.7
  259.5 4.5 fusion.6
  264.0 4.5 fusion.5
  268.4 4.5 fusion.4
  272.9 0.0 reduce-scatter.5.cloned.1.call-update
  272.9 0.2 all-reduce.2.cloned.1.call-start
  273.1 4.3 bitcast_multiply_fusion.2
  277.5 0.0 copy-start.6
  277.5 4.1 multiply_reduce_fusion.1
  281.6 1.3 convolution_convert_fusion.7
  282.9 0.9 copy-done.4
  283.7 1.3 convolution_convert_fusion.6
  285.0 3.6 convolution_convert_fusion.1
  288.6 3.6 convolution_convert_fusion.3
  292.2 3.6 convolution_convert_fusion.5
  295.9 3.6 convolution_convert_fusion
  299.5 3.6 convolution_convert_fusion.2
  303.1 3.6 convolution_convert_fusion.4
  306.7 31.2 %maximum_maximum_fusion = bf16[512,4096]{1,0:T(8,128)(2,1)} fusion(bf16[256,1024]{1,0:T(8,128)(2,1)S(1)} %convolution_convert_fusion, bf16[256,1024]{1,0:T(8,128)(2,1)S(1)} %convolution_convert_fusion.1, bf16[256,1024]{1,0:T(8,128)(2,1)S(1)} %convolution_convert_fusion.2, bf16[256,1024]{1,0:T(8,128)(2,1)S(1)} %convolution_convert_fusion.3, ...), kind=kLoop, calls=%fused_computation.1 | loop fusion | flops 33554432 | bytes 8388608 | tf_op jit(solution)/shard_map/concatenate | solution.py:80
  337.9 0.0 copy-start.9
  337.9 0.0 all-reduce.2.cloned.1.call-update
  337.9 0.0 reduce-scatter.5.cloned.1.call-done
  338.0 0.8 copy-done.9
  338.8 1.6 convert_add_fusion
  340.5 154.6 %all-reduce.2.cloned.1.call-done = bf16[512,4096]{1,0:T(8,128)(2,1)} async-done(((bf16[512,4096]{1,0:T(8,128)(2,1)}), bf16[512,4096]{1,0:T(8,128)(2,1)}) %all-reduce.2.cloned.1.call-update) | async-done | bytes 4194320 | tf_op jit(solution)/shard_map/psum | solution.py:80
  495.1 3.0 multiply_reduce_fusion
  498.1 0.4 copy-done.2
  498.5 3.6 fusion.11
  502.1 1.3 fusion.16
  503.4 3.5 convolution_add_fusion.2
  506.9 3.5 convolution_add_fusion.1
  510.4 3.5 convolution_add_fusion
  513.9 3.5 convolution_add_fusion.5
  517.4 0.0 copy-start.1
  517.4 3.7 convolution_add_fusion.4
  521.1 3.8 fusion.3
  524.9 17.7 %psum.15 = f32[128]{0:T(128)S(1)} all-reduce(f32[128]{0:T(128)S(1)} %bitcast_reduce_fusion), channel_id=1, replica_groups=mesh['dp'=4,'tensor'=8] {'tensor'}, use_global_device_ids=true, to_apply=%region_7.8 | all-reduce | flops 128 | bytes 1024 | tf_op jit(solution)/shard_map/psum | solution.py:86
  542.6 0.5 broadcast_multiply_fusion
  (28 shorter events, 0.1 us)
Async XLA Ops:
  7.2 105.5 %copy-start = (bf16[2,128,4096]{2,1,0:T(8,128)(2,1)S(1)}, bf16[2,128,4096]{2,1,0:T(8,128)(2,1)}, u32[]{:S(2)}) copy-start(bf16[2,128,4096]{2,1,0:T(8,128)(2,1)} %param.13) | copy-start | bytes 6291460
  7.2 194.2 %reduce-scatter.3.cloned.1.call-start = ((), (), s32[]{:S(2)}) async-start(), calls=%async_computation.2 | async-start | bytes 4718592 | tf_op jit(solution)/shard_map/reduce_scatter | solution.py:56
  18.7 225.3 %all-gather.2.cloned.1.call-start = ((), (), s32[]{:S(2)}) async-start(), calls=%async_computation.3 | async-start | bytes 1179648 | tf_op jit(solution)/shard_map/all_gather | solution.py:62
  18.8 93.8 %collective-permute-start.1 = (bf16[1024,2048]{1,0:T(8,128)(2,1)}, bf16[1024,2048]{1,0:T(8,128)(2,1)}, u32[]{:S(2)}, u32[]{:S(2)}) collective-permute-start(bf16[1024,2048]{1,0:T(8,128)(2,1)} %param.11), channel_id=1, source_target_pairs={{16,0},{24,8},{0,16},{8,24},{17,1},{25,9},{1,17},{9,25},{18,2},{26... | collective-permute-start | bytes 12582920 | tf_op jit(solution)/shard_map/ppermute | solution.py:22
  19.4 182.0 %collective-permute-start.4 = (bf16[1024,2048]{1,0:T(8,128)(2,1)}, bf16[1024,2048]{1,0:T(8,128)(2,1)}, u32[]{:S(2)}, u32[]{:S(2)}) collective-permute-start(bf16[1024,2048]{1,0:T(8,128)(2,1)} %param.12), channel_id=1, source_target_pairs={{16,0},{24,8},{0,16},{8,24},{17,1},{25,9},{1,17},{9,25},{18,2},{26... | collective-permute-start | bytes 12582920 | tf_op jit(solution)/shard_map/ppermute | solution.py:22
  20.9 182.9 %collective-permute-start = (bf16[1024,2048]{1,0:T(8,128)(2,1)}, bf16[1024,2048]{1,0:T(8,128)(2,1)}, u32[]{:S(2)}, u32[]{:S(2)}) collective-permute-start(bf16[1024,2048]{1,0:T(8,128)(2,1)} %param.11), channel_id=1, source_target_pairs={{0,8},{8,0},{16,24},{24,16},{1,9},{9,1},{17,25},{25,17},{2,10},{10... | collective-permute-start | bytes 12582920 | tf_op jit(solution)/shard_map/ppermute | solution.py:25
  20.9 192.1 %collective-permute-start.3 = (bf16[1024,2048]{1,0:T(8,128)(2,1)}, bf16[1024,2048]{1,0:T(8,128)(2,1)}, u32[]{:S(2)}, u32[]{:S(2)}) collective-permute-start(bf16[1024,2048]{1,0:T(8,128)(2,1)} %param.12), channel_id=1, source_target_pairs={{0,8},{8,0},{16,24},{24,16},{1,9},{9,1},{17,25},{25,17},{2,10},{10... | collective-permute-start | bytes 12582920 | tf_op jit(solution)/shard_map/ppermute | solution.py:25
  112.6 140.4 %collective-permute-start.2 = (bf16[1024,2048]{1,0:T(8,128)(2,1)}, bf16[1024,2048]{1,0:T(8,128)(2,1)}, u32[]{:S(2)}, u32[]{:S(2)}) collective-permute-start(bf16[1024,2048]{1,0:T(8,128)(2,1)} %collective-permute-done.1), channel_id=1, source_target_pairs={{0,8},{8,0},{16,24},{24,16},{1,9},{9,1},{17,25},{25,17},{2,10},{10... | collective-permute-start | bytes 12582920 | tf_op jit(solution)/shard_map/ppermute | solution.py:25
  112.6 4.9 copy-start.5
  117.6 83.8 %copy-start.11 = (bf16[128,512]{1,0:T(8,128)(2,1)S(1)}, bf16[128,512]{1,0:T(8,128)(2,1)}, u32[]{:S(2)}) copy-start(bf16[128,512]{1,0:T(8,128)(2,1)} %param.10) | copy-start | bytes 393220
  201.4 67.1 %collective-permute-start.5 = (bf16[1024,2048]{1,0:T(8,128)(2,1)}, bf16[1024,2048]{1,0:T(8,128)(2,1)}, u32[]{:S(2)}, u32[]{:S(2)}) collective-permute-start(bf16[1024,2048]{1,0:T(8,128)(2,1)} %collective-permute-done.4), channel_id=1, source_target_pairs={{0,8},{8,0},{16,24},{24,16},{1,9},{9,1},{17,25},{25,17},{2,10},{10... | collective-permute-start | bytes 12582920 | tf_op jit(solution)/shard_map/ppermute | solution.py:25
  203.2 134.7 %reduce-scatter.5.cloned.1.call-start = ((), (), s32[]{:S(2)}) async-start(), calls=%async_computation.4 | async-start | bytes 1179648 | tf_op jit(solution)/shard_map/reduce_scatter | solution.py:95
  208.0 5.0 copy-start.12
  244.0 3.1 copy-start.10
  253.0 4.3 copy-start.3
  272.9 222.1 %all-reduce.2.cloned.1.call-start = ((), (), s32[]{:S(2)}) async-start(), calls=%async_computation.5 | async-start | bytes 8388608 | tf_op jit(solution)/shard_map/psum | solution.py:80
  273.1 4.3 copy-start.8
  277.5 4.1 copy-start.6
  281.6 2.2 copy-start.4
  337.9 0.9 copy-start.9
  495.1 3.4 copy-start.2
  498.5 3.6 copy-start.7
  517.4 25.7 %copy-start.1 = (bf16[2,128,4096]{2,1,0:T(8,128)(2,1)S(1)}, bf16[2,128,4096]{2,1,0:T(8,128)(2,1)}, u32[]{:S(2)}) copy-start(bf16[2,128,4096]{2,1,0:T(8,128)(2,1)} %param.13) | copy-start | bytes 6291460
Sparse Core Ops, SparseCore 0:
  18.9 89.4 reduce-scatter.2
  203.4 40.5 all-gather.1
  273.0 62.8 reduce-scatter.4
  339.5 155.4 all-reduce.1

commit v2 on v1

--- a/solution.py
+++ b/solution.py
@@ -1,6 +1,10 @@
+import functools
+
 import jax
 import jax.numpy as jnp
 from jax import lax
+from jax.experimental import pallas as pl
+from jax.experimental.pallas import tpu as pltpu
 from jax.sharding import PartitionSpec as P
 
 
@@ -38,6 +42,266 @@
     return out
 
 
+def series_kernel(n, nt, nx, n_probes, *refs):
+    w_in, w_out = refs[:n], refs[n : 2 * n]
+    start, mix, slope, u_ref, flowed_ref, log_ref = refs[2 * n : 2 * n + 6]
+    (win, wout, sr, full, sendx, xbuf, own, zbuf, left, right, pbuf, pxbuf, pzbuf,
+     in_sem, out_sem, xs, xr, zs, zr, gs, gr, hs, hr, pxs, pxr, pzs, pzr) = refs[2 * n + 6 :]
+    nz = nt // nx
+    depth, hidden = w_in[0].shape
+    big = start.shape[0]
+    rows = big // n_probes
+    chunk = win.shape[0] // nt
+    tile = min(512, hidden)
+    tiles = hidden // tile
+    t = lax.axis_index("tensor")
+    z, x = lax.div(t, nx), lax.rem(t, nx)
+
+    def dev(zz, xx):
+        return {"tensor": zz * nx + xx}
+
+    def zup(k):
+        return lax.rem(z + k, nz)
+
+    def xup(j):
+        return lax.rem(x + j, nx)
+
+    def remote(src, dst, ss, rs, to):
+        return pltpu.make_async_remote_copy(
+            src_ref=src, dst_ref=dst, send_sem=ss, recv_sem=rs,
+            device_id=to, device_id_type=pl.DeviceIdType.MESH,
+        )
+
+    barrier = pltpu.get_barrier_semaphore()
+    for j in range(1, nx):
+        pl.semaphore_signal(barrier, inc=1, device_id=dev(z, xup(j)), device_id_type=pl.DeviceIdType.MESH)
+    for k in range(1, nz):
+        pl.semaphore_signal(barrier, inc=1, device_id=dev(zup(k), x), device_id_type=pl.DeviceIdType.MESH)
+
+    own_rows = [pl.ds(pl.multiple_of(o * depth, depth), depth) for o in owners(n)]
+    loads_out = [pltpu.make_async_copy(w_out[b], wout.at[own_rows[b]], out_sem.at[b]) for b in range(n)]
+    loads_in = [pltpu.make_async_copy(w_in[b], win.at[own_rows[b]], in_sem.at[b]) for b in range(n)]
+    for c in loads_out + loads_in:
+        c.start()
+
+    def at(i):
+        return pl.ds(pl.multiple_of(i * tile, tile), tile)
+
+    for b in range(n):
+        loads_out[b].wait()
+
+        def pull(i, _):
+            value = dot(start[:, own_rows[b]], wout[own_rows[b], at(i)])
+            right[:, at(i)] = value if b == 0 else right[:, at(i)] + value
+            return 0
+
+        lax.fori_loop(0, tiles, pull, 0)
+    totals = []
+    for p in range(n_probes):
+        band = pl.ds(p * rows, rows)
+
+        def scale(i, acc):
+            r = right[band, at(i)]
+            sr[band, at(i)] = (r * slope[:, at(i)]).astype(jnp.bfloat16)
+            return acc + jnp.sum(mix[band, at(i)].astype(jnp.float32) * r, axis=1, keepdims=True)
+
+        totals.append(lax.fori_loop(0, tiles, scale, jnp.zeros((rows, 1), jnp.float32)))
+    left[...] = jnp.zeros_like(left)
+    right[...] = jnp.zeros_like(right)
+    for c in loads_in:
+        c.wait()
+    pl.semaphore_wait(barrier, nx - 1 + nz - 1)
+
+    def xcopy(s, j):
+        return remote(sendx.at[s, j - 1], xbuf.at[s, j - 1], xs.at[s, j - 1], xr.at[s, j - 1], dev(z, xup(j)))
+
+    def zcopy(s):
+        return remote(own.at[s], zbuf.at[s], zs.at[s], zr.at[s], dev(zup(1 + s), x))
+
+    def finish(s):
+        for j in range(1, nx):
+            xcopy(s, j).wait_recv()
+        for i in range(own.shape[1] // rows):
+            band = pl.ds(i * rows, rows)
+            value = own[s, band, :].astype(jnp.float32)
+            for j in range(1, nx):
+                value += xbuf[s, j - 1, band, :].astype(jnp.float32)
+            own[s, band, :] = value.astype(jnp.bfloat16)
+
+    def scatter(s, _):
+        for j in list(range(1, nx)) + [0]:
+            off = pl.ds(pl.multiple_of((zup(1 + s) * nx + xup(j)) * chunk, chunk), chunk)
+            dst = sendx.at[s, j - 1] if j else own.at[s]
+            dst[pl.ds(0, big), :] = dot_t(sr[...], win[off, :]).astype(jnp.bfloat16)
+            dst[pl.ds(big, big + rows), :] = dot_t(mix[...], wout[off, :]).astype(jnp.bfloat16)
+            if j:
+                xcopy(s, j).start()
+
+        @pl.when(s >= 1)
+        def _():
+            finish(s - 1)
+            zcopy(s - 1).start()
+
+        return 0
+
+    lax.fori_loop(0, nz, scatter, 0)
+    finish(nz - 1)
+    for s in range(nz - 1):
+        zcopy(s).wait_recv()
+    summed = []
+    for i in range(own.shape[1] // rows):
+        band = pl.ds(i * rows, rows)
+        value = own[nz - 1, band, :].astype(jnp.float32)
+        for s in range(nz - 1):
+            value += zbuf[s, band, :].astype(jnp.float32)
+        if i < 2 * n_probes:
+            full[t, band, :] = value.astype(jnp.bfloat16)
+        else:
+            flowed_ref[...] = u_ref[...].astype(jnp.float32) + value
+
+    def gcopy(k):
+        return remote(full.at[t], full.at[t], gs.at[k - 1], gr.at[k - 1], dev(zup(k), x))
+
+    def slot(k, j):
+        return lax.rem(z + nz - k, nz) * nx + lax.rem(x + nx - j, nx)
+
+    def hcopy(k, j):
+        part = full.at[slot(k, 0)]
+        return remote(part, part, hs.at[k, j - 1], hr.at[k, j - 1], dev(z, xup(j)))
+
+    def harrive(k, j):
+        part = full.at[slot(k, j)]
+        return remote(part, part, hs.at[k, j - 1], hr.at[k, j - 1], dev(z, xup(j)))
+
+    def garrive(k):
+        part = full.at[slot(k, 0)]
+        return remote(part, part, gs.at[k - 1], gr.at[k - 1], dev(zup(k), x))
+
+    def consume(c):
+        off = pl.ds(pl.multiple_of(c * chunk, chunk), chunk)
+
+        def body(i, _):
+            left[:, at(i)] += dot(full[c, pl.ds(big, big), :], win[off, at(i)])
+            right[:, at(i)] += dot(full[c, pl.ds(0, big), :], wout[off, at(i)])
+            return 0
+
+        lax.fori_loop(0, tiles, body, 0)
+
+    for k in range(1, nz):
+        gcopy(k).start()
+    for j in range(1, nx):
+        hcopy(0, j).start()
+    for p in range(n_probes):
+        w1 = full[t, pl.ds(p * rows, rows), :].astype(jnp.float32)
+        y1 = full[t, pl.ds(big + p * rows, rows), :].astype(jnp.float32)
+        totals[p] -= 0.5 * jnp.sum(w1 * y1, axis=1, keepdims=True)
+    consume(t)
+
+    def gather(k, _):
+        garrive(k).wait_recv()
+        for j in range(1, nx):
+            hcopy(k, j).start()
+        consume(slot(k, 0))
+        for j in range(1, nx):
+            harrive(k - 1, j).wait_recv()
+            consume(slot(k - 1, j))
+        return 0
+
+    lax.fori_loop(1, nz, gather, 0)
+    for j in range(1, nx):
+        harrive(nz - 1, j).wait_recv()
+        consume(slot(nz - 1, j))
+
+    total = jnp.zeros((rows, 1), jnp.float32)
+    for p in range(n_probes):
+        band = pl.ds(p * rows, rows)
+
+        def last(i, acc):
+            return acc + jnp.sum(left[band, at(i)] * slope[:, at(i)] * right[band, at(i)], axis=1, keepdims=True)
+
+        third = lax.fori_loop(0, tiles, last, jnp.zeros((rows, 1), jnp.float32))
+        total += totals[p] + third / 3.0
+
+    def pxcopy(j):
+        return remote(pbuf.at[0], pxbuf.at[j - 1], pxs.at[j - 1], pxr.at[j - 1], dev(z, xup(j)))
+
+    def pzcopy(k):
+        return remote(pbuf.at[1], pzbuf.at[k - 1], pzs.at[k - 1], pzr.at[k - 1], dev(zup(k), x))
+
+    wide = jnp.broadcast_to(total / n_probes, (rows, 128))
+    pbuf[0] = wide
+    for j in range(1, nx):
+        pxcopy(j).start()
+    for j in range(1, nx):
+        pxcopy(j).wait_recv()
+        wide = wide + pxbuf[j - 1]
+    pbuf[1] = wide
+    for k in range(1, nz):
+        pzcopy(k).start()
+    for k in range(1, nz):
+        pzcopy(k).wait_recv()
+        wide = wide + pzbuf[k - 1]
+    log_ref[...] = wide
+
+    for s in range(nz):
+        for j in range(1, nx):
+            xcopy(s, j).wait_send()
+            hcopy(s, j).wait_send()
+    for k in range(1, nz):
+        zcopy(k - 1).wait_send()
+        gcopy(k).wait_send()
+        pzcopy(k).wait_send()
+    for j in range(1, nx):
+        pxcopy(j).wait_send()
+
+
+def series(n, nt, n_probes, w_in, w_out, start, mix, slope, u_slice):
+    nx = max(2, nt // 4)
+    nz = nt // nx
+    depth, hidden = w_in[0].shape
+    latents = depth * n
+    chunk = latents // nt
+    big = start.shape[0]
+    rows = big // n_probes
+    vmem = pl.BlockSpec(memory_space=pltpu.VMEM)
+    bf, f32 = jnp.bfloat16, jnp.float32
+    dma = pltpu.SemaphoreType.DMA
+    return pl.pallas_call(
+        functools.partial(series_kernel, n, nt, nx, n_probes),
+        out_shape=(jax.ShapeDtypeStruct((rows, chunk), f32), jax.ShapeDtypeStruct((rows, 128), f32)),
+        in_specs=[pl.BlockSpec(memory_space=pl.ANY)] * (2 * n) + [vmem] * 4,
+        out_specs=(vmem, vmem),
+        scratch_shapes=[
+            pltpu.VMEM((latents, hidden), bf),
+            pltpu.VMEM((latents, hidden), bf),
+            pltpu.VMEM((big, hidden), bf),
+            pltpu.VMEM((nt, 2 * big, chunk), bf),
+            pltpu.VMEM((nz, nx - 1, 2 * big + rows, chunk), bf),
+            pltpu.VMEM((nz, nx - 1, 2 * big + rows, chunk), bf),
+            pltpu.VMEM((nz, 2 * big + rows, chunk), bf),
+            pltpu.VMEM((nz - 1, 2 * big + rows, chunk), bf),
+            pltpu.VMEM((big, hidden), f32),
+            pltpu.VMEM((big, hidden), f32),
+            pltpu.VMEM((2, rows, 128), f32),
+            pltpu.VMEM((nx - 1, rows, 128), f32),
+            pltpu.VMEM((nz - 1, rows, 128), f32),
+            dma((n,)), dma((n,)),
+            dma((nz, nx - 1)), dma((nz, nx - 1)),
+            dma((nz - 1,)), dma((nz - 1,)),
+            dma((nz - 1,)), dma((nz - 1,)),
+            dma((nz, nx - 1)), dma((nz, nx - 1)),
+            dma((nx - 1,)), dma((nx - 1,)),
+            dma((nz - 1,)), dma((nz - 1,)),
+        ],
+        compiler_params=pltpu.CompilerParams(
+            collective_id=0, has_side_effects=True, vmem_limit_bytes=61 * 1024 * 1024
+        ),
+        cost_estimate=pl.CostEstimate(
+            flops=2 * big * latents * hidden * 6, bytes_accessed=4 * latents * hidden, transcendentals=0
+        ),
+    )(*w_in, *w_out, start, mix, slope, u_slice)
+
+
 def make_local(n, t):
     def local(features, enc_in, enc_out, noise, in_weight, out_weight, probes):
         rows = features.shape[0]
@@ -66,36 +330,15 @@
         pre_act = sum(dot(a, w) for a, w in zip(cols(u_full), w_in))
         tanh_val = jnp.tanh(pre_act)
         squash = tanh_val.astype(jnp.bfloat16)
-        slope = jnp.tile(1.0 - tanh_val * tanh_val, (n_probes, 1))
-        sq = q * slope
-        sq16 = sq.astype(jnp.bfloat16)
-        r = sum(dot(a, w) for a, w in zip(start, w_out))
-        sr16 = (r * slope).astype(jnp.bfloat16)
-        first = jnp.sum(sq * r, axis=1)
-
-        both = [
-            jnp.concatenate([dot_t(sr16, wi), dot_t(sq16, wo)], 0).astype(jnp.bfloat16)
-            for wi, wo in zip(w_in, w_out)
+        slope = 1.0 - tanh_val * tanh_val
+        scaled = [
+            (q[p * rows : (p + 1) * rows] * slope).astype(jnp.bfloat16) for p in range(n_probes)
         ]
-        both = lax.psum(jnp.concatenate(both, 1), "tensor")
-        w1, y1 = both[: n_probes * rows], both[n_probes * rows :]
-        second = jnp.sum(w1.astype(jnp.float32) * y1.astype(jnp.float32), axis=1) / t
-        left = sum(dot(y1[:, i * depth : (i + 1) * depth], w) for i, w in enumerate(w_in))
-        right = sum(dot(w1[:, i * depth : (i + 1) * depth], w) for i, w in enumerate(w_out))
-        third = jnp.sum(left * slope * right, axis=1)
-        logdet = lax.psum(
-            jnp.sum((first - second / 2 + third / 3).reshape(n_probes, rows), 0), "tensor"
-        ) / n_probes
-
-        branch = jnp.zeros((rows, latents), jnp.bfloat16)
-        for o, w in zip(own, w_out):
-            branch = lax.dynamic_update_slice_in_dim(
-                branch, dot_t(squash, w).astype(jnp.bfloat16), o * depth, 1
-            )
-        flowed = u_slice.astype(jnp.float32) + lax.psum_scatter(
-            branch, "tensor", scatter_dimension=1, tiled=True
-        ).astype(jnp.float32)
-        return flowed, logdet
+        flowed, logdet = series(
+            n, t, n_probes, w_in, w_out, probes.reshape(n_probes * rows, latents),
+            jnp.concatenate(scaled + [squash], 0), slope, u_slice,
+        )
+        return flowed, logdet[:, 0]
 
     return local
 

time: 558 us -> 454 us (0.81)
  Pallas kernels: 0 us -> 178 us
  waiting for transfers between devices: 350 us -> 205 us
  matrix products: 119 us -> 35.7 us
  other arithmetic: 38.2 us -> 3.24 us
  blocking collectives: 17.7 us -> 0 us
    pallas_call x0 -> x1, Pallas kernels: none -> 178 us  [series(): pl.pallas_call(functools.partial(series_kernel, n, nt, nx, n_probes), out...]
    psum x1 -> x0, waiting for transfers between devices: 155 us -> none  [local(): both = lax.psum(jnp.concatenate(both, 1), 'tensor')]
    dot_general x21 -> x9, matrix products: 78.7 us -> 35.7 us  [dot(): return jnp.dot(a, b, preferred_element_type=jnp.float32)]
    dot_general x12 -> x0, matrix products: 39.8 us -> none  [dot_t(): lax.dot_general(a, b, (((1,), (1,)), ((), ())), preferred_element_type=jn...]
    concatenate x1, other arithmetic: 31.2 us -> 1.39 us  [local(): jnp.concatenate(scaled + [squash], 0)]
    psum x1 -> x0, blocking collectives: 17.7 us -> none  [local(): lax.psum(jnp.sum((first - second / 2 + third / 3).reshape(n_probes, rows)...]
    ppermute x2, waiting for transfers between devices: 172 us -> 180 us  [gather_blocks(): lax.ppermute(shard, 'dp', [((y + k) % half * 2 + c, y * 2 + c) for y in r...]
  transfers between devices with their start and end apart: 10 -> 8, of which waited for: 4 -> 3; matrix products, arithmetic and copies ran while one was open for 21% -> 7% of each run, Pallas kernels for 0% -> 0%
where the time goes in v2:
time: 454 us; the launch traced here: 449 us
  waiting for transfers between devices  205 us (45%)
  Pallas kernels  178 us (39%)
  matrix products  35.7 us (8%)
  between operations  14.2 us (3%)
  local copies, waits for them, and re-layouts  10.3 us (2%)
    ppermute x2, waiting for transfers between devices, gather_blocks(): lax.ppermute(shard, 'dp', [((y + k) % half * 2 + c, y * 2 + c) for y in r...  180 us
    pallas_call x1, Pallas kernels, series(): pl.pallas_call(functools.partial(series_kernel, n, nt, nx, n_probes), out...  178 us
    dot_general x9, matrix products, dot(): return jnp.dot(a, b, preferred_element_type=jnp.float32)  35.7 us
    all_gather x1, waiting for transfers between devices, local(): u_full = lax.all_gather(u_slice, 'tensor', axis=1, tiled=True)  24.8 us
  transfers between devices with their start and end apart: 8, of which 3 were waited for; matrix products, arithmetic and copies ran while one was open for 7% of the time, Pallas kernels for 0%

profile of v2, /device:TPU:6, one launch (start us, length us, event | category | flops | bytes accessed | tf_op | source)
XLA Modules:
  0.0 449.3 jit_solution(3001222475086347030)
XLA Ops:
  7.2 0.0 copy-start
  7.2 0.0 reduce-scatter.2.cloned.1.call-start
  7.2 1.5 copy-done
  8.8 6.7 %fusion.16 = f32[128,8192]{0,1:T(8,128)} fusion(bf16[256,8192]{1,0:T(8,128)(2,1)} %param.9, bf16[128,4096]{1,0:T(8,128)(2,1)} %param.7, bf16[4096,256]{1,0:T(8,128)(2,1)S(1)} %copy-done), kind=kOutput, calls=%fused_computation.30 | convolution fusion | flops 805470208 | bytes 11534336 | tf_op jit(solution)/shard_map/dot_general | solution.py:12
  15.4 5.6 %copy.10 = f32[128,2,4096]{2,0,1:T(8,128)} copy(f32[128,2,4096]{0,2,1:T(8,128)} %bitcast.21) | data formatting | bytes 8388608 | tf_op jit(solution)/shard_map/reshape | solution.py:321
  21.0 0.0 copy-start.4
  21.0 0.0 reduce-scatter.2.cloned.1.call-update
  21.1 0.0 all-gather.2.cloned.1.call-start
  21.1 0.6 collective-permute-start.1
  21.7 1.5 collective-permute-start.4
  23.2 0.0 collective-permute-start
  23.2 91.7 %collective-permute-done.1.refs_2_ = bf16[1024,2048]{1,0:T(8,128)(2,1)} collective-permute-done((bf16[1024,2048]{1,0:T(8,128)(2,1)}, bf16[1024,2048]{1,0:T(8,128)(2,1)}, u32[]{:S(2)}, u32[]{:S(2)}) %collective-permute-start.1) | collective-permute-done | bytes 4194336 | tf_op jit(solution)/shard_map/ppermute | solution.py:26
  115.0 0.0 collective-permute-start.2
  115.0 0.5 collective-permute-start.3
  115.5 88.2 %collective-permute-done.4.refs_6_ = bf16[1024,2048]{1,0:T(8,128)(2,1)} collective-permute-done((bf16[1024,2048]{1,0:T(8,128)(2,1)}, bf16[1024,2048]{1,0:T(8,128)(2,1)}, u32[]{:S(2)}, u32[]{:S(2)}) %collective-permute-start.4) | collective-permute-done | bytes 4194336 | tf_op jit(solution)/shard_map/ppermute | solution.py:26
  203.7 0.0 collective-permute-start.5
  203.7 0.0 reduce-scatter.2.cloned.1.call-done
  203.7 0.0 copy-done.4
  203.7 1.9 fusion.10.refs_11_
  205.6 0.0 all-gather.2.cloned.1.call-update
  205.6 3.6 fusion.6
  209.2 0.0 copy-start.5
  209.3 0.0 collective-permute-done.refs_1_
  209.3 3.8 convolution_add_fusion.2
  213.1 0.0 copy-done.5
  213.1 3.6 convolution_add_fusion.1
  216.7 0.0 collective-permute-done.2.refs_3_
  216.7 4.9 %convolution_add_fusion = f32[256,2048]{1,0:T(8,128)} fusion(f32[256,2048]{1,0:T(8,128)S(1)} %convolution_add_fusion.1, bf16[1024,2048]{1,0:T(8,128)(2,1)} %collective-permute-done.2.refs_3_, bf16[256,4096]{1,0:T(8,128)(2,1)S(1)} %bitcast.26, s32[]{:T(128)S(6)} %select_n.23), kind=kOutput, calls=%fused_computation | convolution fusion | flops 1074266112 | bytes 8912900 | tf_op jit(solution)/shard_map/dot_general | solution.py:12
  221.6 24.8 %all-gather.2.cloned.1.call-done = bf16[128,4096]{1,0:T(8,128)(2,1)} async-done(((bf16[128,512]{1,0:T(8,128)(2,1)}), bf16[128,4096]{1,0:T(8,128)(2,1)}) %all-gather.2.cloned.1.call-update) | async-done | bytes 1048592 | tf_op jit(solution)/shard_map/all_gather | solution.py:326
  246.3 0.0 copy-start.2
  246.3 3.1 fusion.14
  249.4 0.0 copy-done.2
  249.4 2.9 convolution_add_fusion.5
  252.4 0.0 copy-start.3
  252.4 3.1 convolution_add_fusion.4
  255.5 0.0 copy-done.3
  255.5 4.1 fusion.2
  259.6 1.4 pad_maximum_fusion.refs_9_
  261.0 0.0 collective-permute-done.3.refs_5_
  261.0 0.0 collective-permute-done.5.refs_7_
  261.0 0.0 copy-start.1
  261.0 178.3 %shard_map.86 = (f32[128,512]{1,0:T(8,128)}, f32[128,128]{1,0:T(8,128)}) custom-call(bf16[1024,2048]{1,0:T(8,128)(2,1)} %refs_0_.1, bf16[1024,2048]{1,0:T(8,128)(2,1)} %collective-permute-done.refs_1_, bf16[1024,2048]{1,0:T(8,128)(2,1)} %collective-permute-done.1.refs_2_, bf16[1024,2048]{1,0:T(8,128)(2,1)} %collective-permute-done.2.refs_3_, ...), custom_call_target="tpu_custom_call" | custom-call | flops 25769803776 | bytes 33554432 | tf_op jit(solution)/shard_map/pallas_call | solution.py:269
  439.3 1.5 slice_reduce_fusion
  440.8 1.7 copy.13
  442.5 0.0 copy-done.1
Async XLA Ops:
  7.2 1.6 copy-start
  7.2 196.5 %reduce-scatter.2.cloned.1.call-start = ((), (), s32[]{:S(2)}) async-start(), calls=%async_computation.1 | async-start | bytes 4718592 | tf_op jit(solution)/shard_map/reduce_scatter | solution.py:320
  21.0 182.7 %copy-start.4 = (bf16[128,512]{1,0:T(8,128)(2,1)S(1)}, bf16[128,512]{1,0:T(8,128)(2,1)}, u32[]{:S(2)}) copy-start(bf16[128,512]{1,0:T(8,128)(2,1)} %param.10) | copy-start | bytes 393220
  21.1 225.3 %all-gather.2.cloned.1.call-start = ((), (), s32[]{:S(2)}) async-start(), calls=%async_computation.2 | async-start | bytes 1179648 | tf_op jit(solution)/shard_map/all_gather | solution.py:326
  21.1 93.8 %collective-permute-start.1 = (bf16[1024,2048]{1,0:T(8,128)(2,1)}, bf16[1024,2048]{1,0:T(8,128)(2,1)}, u32[]{:S(2)}, u32[]{:S(2)}) collective-permute-start(bf16[1024,2048]{1,0:T(8,128)(2,1)} %refs_0_.1), channel_id=1, source_target_pairs={{16,0},{24,8},{0,16},{8,24},{17,1},{25,9},{1,17},{9,25},{18,2},{26... | collective-permute-start | bytes 12582920 | tf_op jit(solution)/shard_map/ppermute | solution.py:26
  21.7 182.0 %collective-permute-start.4 = (bf16[1024,2048]{1,0:T(8,128)(2,1)}, bf16[1024,2048]{1,0:T(8,128)(2,1)}, u32[]{:S(2)}, u32[]{:S(2)}) collective-permute-start(bf16[1024,2048]{1,0:T(8,128)(2,1)} %refs_4_.1), channel_id=1, source_target_pairs={{16,0},{24,8},{0,16},{8,24},{17,1},{25,9},{1,17},{9,25},{18,2},{26... | collective-permute-start | bytes 12582920 | tf_op jit(solution)/shard_map/ppermute | solution.py:26
  23.2 186.1 %collective-permute-start = (bf16[1024,2048]{1,0:T(8,128)(2,1)}, bf16[1024,2048]{1,0:T(8,128)(2,1)}, u32[]{:S(2)}, u32[]{:S(2)}) collective-permute-start(bf16[1024,2048]{1,0:T(8,128)(2,1)} %refs_0_.1), channel_id=1, source_target_pairs={{0,8},{8,0},{16,24},{24,16},{1,9},{9,1},{17,25},{25,17},{2,10},{10... | collective-permute-start | bytes 12582920 | tf_op jit(solution)/shard_map/ppermute | solution.py:29
  115.0 101.7 %collective-permute-start.2 = (bf16[1024,2048]{1,0:T(8,128)(2,1)}, bf16[1024,2048]{1,0:T(8,128)(2,1)}, u32[]{:S(2)}, u32[]{:S(2)}) collective-permute-start(bf16[1024,2048]{1,0:T(8,128)(2,1)} %collective-permute-done.1.refs_2_), channel_id=1, source_target_pairs={{0,8},{8,0},{16,24},{24,16},{1,9},{9,1},{17,25},{25,17},{2,10},{10... | collective-permute-start | bytes 12582920 | tf_op jit(solution)/shard_map/ppermute | solution.py:29
  115.0 146.0 %collective-permute-start.3 = (bf16[1024,2048]{1,0:T(8,128)(2,1)}, bf16[1024,2048]{1,0:T(8,128)(2,1)}, u32[]{:S(2)}, u32[]{:S(2)}) collective-permute-start(bf16[1024,2048]{1,0:T(8,128)(2,1)} %refs_4_.1), channel_id=1, source_target_pairs={{0,8},{8,0},{16,24},{24,16},{1,9},{9,1},{17,25},{25,17},{2,10},{10... | collective-permute-start | bytes 12582920 | tf_op jit(solution)/shard_map/ppermute | solution.py:29
  203.7 57.3 %collective-permute-start.5 = (bf16[1024,2048]{1,0:T(8,128)(2,1)}, bf16[1024,2048]{1,0:T(8,128)(2,1)}, u32[]{:S(2)}, u32[]{:S(2)}) collective-permute-start(bf16[1024,2048]{1,0:T(8,128)(2,1)} %collective-permute-done.4.refs_6_), channel_id=1, source_target_pairs={{0,8},{8,0},{16,24},{24,16},{1,9},{9,1},{17,25},{25,17},{2,10},{10... | collective-permute-start | bytes 12582920 | tf_op jit(solution)/shard_map/ppermute | solution.py:29
  209.2 3.8 copy-start.5
  246.3 3.1 copy-start.2
  252.4 3.1 copy-start.3
  261.0 181.5 %copy-start.1 = (bf16[4096,256]{1,0:T(8,128)(2,1)S(1)}, bf16[4096,256]{1,0:T(8,128)(2,1)}, u32[]{:S(2)}) copy-start(bf16[4096,256]{1,0:T(8,128)(2,1)} %param.8) | copy-start | bytes 6291460
Sparse Core Ops, SparseCore 0:
  21.2 89.6 reduce-scatter.1
  205.7 40.5 all-gather.1

commit v3 on v2

v3 whole, which is shorter than its diff:
```python
import functools

import jax
import jax.numpy as jnp
from jax import lax
from jax.experimental import pallas as pl
from jax.experimental.pallas import tpu as pltpu
from jax.sharding import PartitionSpec as P


def dot(a, b):
    return jnp.dot(a, b, preferred_element_type=jnp.float32)


def dot_t(a, b):
    return lax.dot_general(a, b, (((1,), (1,)), ((), ())), preferred_element_type=jnp.float32)


def gather_blocks(shard, n):
    half = n // 2
    swap = [(d, d ^ 1) for d in range(n)]
    blocks = []
    for k in range(half):
        own = shard
        if k:
            own = lax.ppermute(
                shard, "dp", [(((y + k) % half) * 2 + c, y * 2 + c) for y in range(half) for c in range(2)]
            )
        blocks += [own, lax.ppermute(own, "dp", swap)]
    return blocks


def owners(n):
    me = lax.axis_index("dp")
    core = lax.rem(me, 2)
    y = lax.div(me, 2)
    half = n // 2
    out = []
    for k in range(half):
        yk = lax.rem(y + k, half)
        out += [yk * 2 + core, yk * 2 + 1 - core]
    return out


def series_kernel(n, nt, nx, n_probes, *refs):
    w_in = refs[:n]
    w_shard, lhs, u_ref, flowed_ref, log_ref = refs[n : n + 5]
    (win, wout, sr, mix, slope, full, sendx, xbuf, own, zbuf, left, right, pbuf, pxbuf, pzbuf,
     in_sem, out_sem, ys, yr, fs, fr, cs, cr,
     xs, xr, zs, zr, gs, gr, hs, hr, pxs, pxr, pzs, pzr) = refs[n + 5 :]
    nz = nt // nx
    half = n // 2
    depth, hidden = w_in[0].shape
    big, rows = sr.shape[0], slope.shape[0]
    chunk = win.shape[0] // nt
    pieces = depth // chunk
    tile = min(512, hidden)
    tiles = hidden // tile
    t = lax.axis_index("tensor")
    z, x = lax.div(t, nx), lax.rem(t, nx)
    me = lax.axis_index("dp")
    y, core = lax.div(me, 2), lax.rem(me, 2)
    mate = {"dp": y * 2 + 1 - core}
    held = owners(n)
    mesh_ids = pl.DeviceIdType.MESH
    W, M = 0, 1
    bands = (pl.ds(0, big), pl.ds(big, big + rows))
    gbands = (pl.ds(0, big), pl.ds(big, big))

    def dev(zz, xx):
        return {"tensor": zz * nx + xx}

    def zup(k):
        return lax.rem(z + k, nz)

    def xup(j):
        return lax.rem(x + j, nx)

    def remote(src, dst, ss, rs, to):
        return pltpu.make_async_remote_copy(
            src_ref=src, dst_ref=dst, send_sem=ss, recv_sem=rs, device_id=to, device_id_type=mesh_ids
        )

    def at(i):
        return pl.ds(pl.multiple_of(i * tile, tile), tile)

    def block(o):
        return pl.ds(pl.multiple_of(o * depth, depth), depth)

    def piece(o, p):
        return pl.ds(pl.multiple_of(o * depth + p * chunk, chunk), chunk)

    barrier = pltpu.get_barrier_semaphore()
    peers = [dev(z, xup(j)) for j in range(1, nx)] + [dev(zup(k), x) for k in range(1, nz)]
    peers += [{"dp": lax.rem(y + k, half) * 2 + core} for k in range(1, half)] + [mate]
    for peer in peers:
        pl.semaphore_signal(barrier, inc=1, device_id=peer, device_id_type=mesh_ids)
    pl.semaphore_wait(barrier, len(peers))

    def ycopy(k, p):
        return remote(
            w_shard.at[pl.ds(p * chunk, chunk)], wout.at[piece(me, p)], ys.at[k - 1, p], yr.at[k - 1, p],
            {"dp": lax.rem(y + half - k, half) * 2 + core},
        )

    def yarrive(k, p):
        part = wout.at[piece(held[2 * k], p)]
        return remote(part, part, ys.at[k - 1, p], yr.at[k - 1, p], mate)

    def fcopy(k, p, own_side=True):
        part = wout.at[piece(held[2 * k + (0 if own_side else 1)], p)]
        return remote(part, part, fs.at[k - 1, p], fr.at[k - 1, p], mate)

    def ccopy(o):
        return remote(w_shard, wout.at[block(o)], cs, cr, mate)

    for k in range(1, half):
        ycopy(k, 0).start()
    loads_in = [pltpu.make_async_copy(w_in[b], win.at[block(held[b])], in_sem.at[b]) for b in range(n)]
    for c in loads_in:
        c.start()
    load_out = pltpu.make_async_copy(w_shard, wout.at[block(me)], out_sem)
    load_out.start()
    ccopy(me).start()

    for b in range(n):
        loads_in[b].wait()

        def first_pass(i, _):
            value = dot(lhs[:, block(held[b])], win[block(held[b]), at(i)])
            left[:, at(i)] = value[:big] if b == 0 else left[:, at(i)] + value[:big]
            slope[:, at(i)] = value[big:] if b == 0 else slope[:, at(i)] + value[big:]
            return 0

        lax.fori_loop(0, tiles, first_pass, 0)
        if b == n // 2:
            for k in range(1, half):
                for p in range(1, pieces):
                    ycopy(k, p).start()

    def activate(i, _):
        th = jnp.tanh(slope[:, at(i)])
        mix[pl.ds(big, rows), at(i)] = th.astype(jnp.bfloat16)
        s = 1.0 - th * th
        slope[:, at(i)] = s
        for p in range(n_probes):
            band = pl.ds(p * rows, rows)
            mix[band, at(i)] = (left[band, at(i)] * s).astype(jnp.bfloat16)
        return 0

    lax.fori_loop(0, tiles, activate, 0)
    left[...] = jnp.zeros_like(left)
    right[...] = jnp.zeros_like(right)

    def xcopy(kind, zt, j):
        band = bands[kind]
        return remote(
            sendx.at[zt, j - 1, band], xbuf.at[zt, j - 1, band],
            xs.at[kind, zt, j - 1], xr.at[kind, zt, j - 1], dev(z, xup(j)),
        )

    def zcopy(kind, k):
        band = bands[kind]
        return remote(
            own.at[zup(k), band], zbuf.at[k - 1, band], zs.at[kind, k - 1], zr.at[kind, k - 1], dev(zup(k), x)
        )

    def finish(kind, zt):
        for j in range(1, nx):
            xcopy(kind, zt, j).wait_recv()
        for i in range(bands[kind].size // rows):
            band = pl.ds(bands[kind].start + i * rows, rows)
            value = own[zt, band, :].astype(jnp.float32)
            for j in range(1, nx):
                value += xbuf[zt, j - 1, band, :].astype(jnp.float32)
            own[zt, band, :] = value.astype(jnp.bfloat16)

        @pl.when(zt != z)
        def _():
            zcopy(kind, lax.rem(zt - z + nz, nz)).start()

    def summed(kind):
        for k in range(1, nz):
            zcopy(kind, k).wait_recv()
        for i in range(bands[kind].size // rows):
            band = pl.ds(bands[kind].start + i * rows, rows)
            value = own[z, band, :].astype(jnp.float32)
            for k in range(1, nz):
                value += zbuf[k - 1, band, :].astype(jnp.float32)
            if kind == M and i == n_probes:
                flowed_ref[...] = u_ref[...].astype(jnp.float32) + value
            else:
                full[t, band, :] = value.astype(jnp.bfloat16)

    def process(o, p):
        off = piece(o, p)

        def pull(i, _):
            right[:, at(i)] += dot(lhs[pl.ds(0, big), off], wout[off, at(i)])
            return 0

        lax.fori_loop(0, tiles, pull, 0)
        target = o * pieces + p
        zt, xt = lax.div(target, nx), lax.rem(target, nx)
        jj = lax.rem(xt - x + nx, nx)
        value = dot_t(mix[...], wout[off, :]).astype(jnp.bfloat16)

        @pl.when(jj == 0)
        def _():
            own[zt, bands[M], :] = value

        @pl.when(jj != 0)
        def _():
            sendx[zt, jj - 1, bands[M], :] = value
            xcopy(M, zt, jj).start()

    def whole_block(o):
        def body(p, _):
            process(o, p)
            return 0

        lax.fori_loop(0, pieces, body, 0)

    def group_rows(k):
        a, b = held[2 * k], held[2 * k + 1]
        return [a, b] if n == nz else [lax.div(a, n // nz)]

    load_out.wait()
    whole_block(me)
    ccopy(held[1]).wait_recv()
    whole_block(held[1])
    for k in range(1, half):
        for p in range(pieces):
            yarrive(k, p).wait_recv()
            fcopy(k, p).start()
            if p == 0:
                for zt in group_rows(k - 1):
                    finish(M, zt)
            process(held[2 * k], p)
            fcopy(k, p, False).wait_recv()
            process(held[2 * k + 1], p)

    totals = []
    for p in range(n_probes):
        band = pl.ds(p * rows, rows)

        def scale(i, acc):
            r = right[band, at(i)]
            sr[band, at(i)] = (r * slope[:, at(i)]).astype(jnp.bfloat16)
            return acc + jnp.sum(mix[band, at(i)].astype(jnp.float32) * r, axis=1, keepdims=True)

        totals.append(lax.fori_loop(0, tiles, scale, jnp.zeros((rows, 1), jnp.float32)))
    right[...] = jnp.zeros_like(right)

    def scatter(s, _):
        zt = zup(1 + s)
        for j in list(range(1, nx)) + [0]:
            off = pl.ds(pl.multiple_of((zt * nx + xup(j)) * chunk, chunk), chunk)
            value = dot_t(sr[...], win[off, :]).astype(jnp.bfloat16)
            if j:
                sendx[zt, j - 1, bands[W], :] = value
                xcopy(W, zt, j).start()
            else:
                own[zt, bands[W], :] = value

        @pl.when(s == 0)
        def _():
            for zz in group_rows(half - 1):
                finish(M, zz)

        @pl.when(s >= 1)
        def _():
            finish(W, zup(s))

        return 0

    lax.fori_loop(0, nz, scatter, 0)

    def gcopy(kind, k):
        part = full.at[t, gbands[kind]]
        return remote(part, part, gs.at[kind, k - 1], gr.at[kind, k - 1], dev(zup(k), x))

    def slot(k, j):
        return lax.rem(z + nz - k, nz) * nx + lax.rem(x + nx - j, nx)

    def garrive(kind, k):
        part = full.at[slot(k, 0), gbands[kind]]
        return remote(part, part, gs.at[kind, k - 1], gr.at[kind, k - 1], dev(zup(k), x))

    def hcopy(kind, k, j):
        part = full.at[slot(k, 0), gbands[kind]]
        return remote(part, part, hs.at[kind, k, j - 1], hr.at[kind, k, j - 1], dev(z, xup(j)))

    def harrive(kind, k, j):
        part = full.at[slot(k, j), gbands[kind]]
        return remote(part, part, hs.at[kind, k, j - 1], hr.at[kind, k, j - 1], dev(z, xup(j)))

    def consume(kind, c):
        off = pl.ds(pl.multiple_of(c * chunk, chunk), chunk)
        acc, weight = (left, win) if kind == M else (right, wout)

        def body(i, _):
            acc[:, at(i)] += dot(full[c, gbands[kind], :], weight[off, at(i)])
            return 0

        lax.fori_loop(0, tiles, body, 0)

    def send_own(kind):
        for k in range(1, nz):
            gcopy(kind, k).start()
        for j in range(1, nx):
            hcopy(kind, 0, j).start()

    summed(M)
    send_own(M)
    finish(W, z)
    consume(M, t)
    summed(W)
    send_own(W)
    for p in range(n_probes):
        w1 = full[t, pl.ds(p * rows, rows), :].astype(jnp.float32)
        y1 = full[t, pl.ds(big + p * rows, rows), :].astype(jnp.float32)
        totals[p] -= 0.5 * jnp.sum(w1 * y1, axis=1, keepdims=True)
    consume(W, t)

    def gather(k, _):
        for kind in (M, W):
            garrive(kind, k).wait_recv()
            for j in range(1, nx):
                hcopy(kind, k, j).start()
            consume(kind, slot(k, 0))
        for kind in (M, W):
            for j in range(1, nx):
                harrive(kind, k - 1, j).wait_recv()
                consume(kind, slot(k - 1, j))
        return 0

    lax.fori_loop(1, nz, gather, 0)
    for kind in (M, W):
        for j in range(1, nx):
            harrive(kind, nz - 1, j).wait_recv()
            consume(kind, slot(nz - 1, j))

    total = jnp.zeros((rows, 1), jnp.float32)
    for p in range(n_probes):
        band = pl.ds(p * rows, rows)

        def last(i, acc):
            return acc + jnp.sum(left[band, at(i)] * slope[:, at(i)] * right[band, at(i)], axis=1, keepdims=True)

        third = lax.fori_loop(0, tiles, last, jnp.zeros((rows, 1), jnp.float32))
        total += totals[p] + third / 3.0

    def pxcopy(j):
        return remote(pbuf.at[0], pxbuf.at[j - 1], pxs.at[j - 1], pxr.at[j - 1], dev(z, xup(j)))

    def pzcopy(k):
        return remote(pbuf.at[1], pzbuf.at[k - 1], pzs.at[k - 1], pzr.at[k - 1], dev(zup(k), x))

    wide = jnp.broadcast_to(total / n_probes, (rows, 128))
    pbuf[0] = wide
    for j in range(1, nx):
        pxcopy(j).start()
    for j in range(1, nx):
        pxcopy(j).wait_recv()
        wide = wide + pxbuf[j - 1]
    pbuf[1] = wide
    for k in range(1, nz):
        pzcopy(k).start()
    for k in range(1, nz):
        pzcopy(k).wait_recv()
        wide = wide + pzbuf[k - 1]
    log_ref[...] = wide

    for kind in (W, M):
        for s in range(nz):
            for j in range(1, nx):
                xcopy(kind, s, j).wait_send()
                hcopy(kind, s, j).wait_send()
        for k in range(1, nz):
            zcopy(kind, k).wait_send()
            gcopy(kind, k).wait_send()
    for k in range(1, nz):
        pzcopy(k).wait_send()
    for j in range(1, nx):
        pxcopy(j).wait_send()
    ccopy(me).wait_send()
    for k in range(1, half):
        for p in range(pieces):
            ycopy(k, p).wait_send()
            fcopy(k, p).wait_send()


def series(n, nt, n_probes, w_in, w_shard, lhs, u_slice):
    nx = max(2, nt // 4)
    nz = nt // nx
    depth, hidden = w_in[0].shape
    latents = depth * n
    chunk = latents // nt
    pieces = depth // chunk
    rows = u_slice.shape[0]
    big = n_probes * rows
    half = n // 2
    vmem = pl.BlockSpec(memory_space=pltpu.VMEM)
    bf, f32 = jnp.bfloat16, jnp.float32
    dma = pltpu.SemaphoreType.DMA
    return pl.pallas_call(
        functools.partial(series_kernel, n, nt, nx, n_probes),
        out_shape=(jax.ShapeDtypeStruct((rows, chunk), f32), jax.ShapeDtypeStruct((rows, 128), f32)),
        in_specs=[pl.BlockSpec(memory_space=pl.ANY)] * (n + 1) + [vmem] * 2,
        out_specs=(vmem, vmem),
        scratch_shapes=[
            pltpu.VMEM((latents, hidden), bf),
            pltpu.VMEM((latents, hidden), bf),
            pltpu.VMEM((big, hidden), bf),
            pltpu.VMEM((big + rows, hidden), bf),
            pltpu.VMEM((rows, hidden), f32),
            pltpu.VMEM((nt, 2 * big, chunk), bf),
            pltpu.VMEM((nz, nx - 1, 2 * big + rows, chunk), bf),
            pltpu.VMEM((nz, nx - 1, 2 * big + rows, chunk), bf),
            pltpu.VMEM((nz, 2 * big + rows, chunk), bf),
            pltpu.VMEM((nz - 1, 2 * big + rows, chunk), bf),
            pltpu.VMEM((big, hidden), f32),
            pltpu.VMEM((big, hidden), f32),
            pltpu.VMEM((2, rows, 128), f32),
            pltpu.VMEM((nx - 1, rows, 128), f32),
            pltpu.VMEM((nz - 1, rows, 128), f32),
            dma((n,)), dma,
            dma((half - 1, pieces)), dma((half - 1, pieces)),
            dma((half - 1, pieces)), dma((half - 1, pieces)),
            dma, dma,
            dma((2, nz, nx - 1)), dma((2, nz, nx - 1)),
            dma((2, nz - 1)), dma((2, nz - 1)),
            dma((2, nz - 1)), dma((2, nz - 1)),
            dma((2, nz, nx - 1)), dma((2, nz, nx - 1)),
            dma((nx - 1,)), dma((nx - 1,)),
            dma((nz - 1,)), dma((nz - 1,)),
        ],
        compiler_params=pltpu.CompilerParams(
            collective_id=0, has_side_effects=True, vmem_limit_bytes=62 * 1024 * 1024
        ),
        cost_estimate=pl.CostEstimate(
            flops=2 * big * latents * hidden * 6, bytes_accessed=4 * latents * hidden, transcendentals=0
        ),
    )(*w_in, w_shard, lhs, u_slice)


def make_local(n, t):
    def local(features, enc_in, enc_out, noise, in_weight, out_weight, probes):
        rows = features.shape[0]
        depth = in_weight.shape[0]
        latents = depth * n
        n_probes = probes.shape[0]
        w_in = gather_blocks(in_weight, n)
        hidden = jax.nn.silu(dot(features, enc_in)).astype(jnp.bfloat16)
        partial_stats = dot(hidden, enc_out)
        moments = lax.psum_scatter(
            partial_stats.astype(jnp.bfloat16).reshape(rows, 2, latents), "tensor", scatter_dimension=2, tiled=True
        )
        moments = moments.astype(jnp.float32)
        u_slice = (
            moments[:, 0] + jax.nn.softplus(moments[:, 1]) * noise.astype(jnp.float32)
        ).astype(jnp.bfloat16)
        u_full = lax.all_gather(u_slice, "tensor", axis=1, tiled=True)

        lhs = jnp.concatenate([probes.reshape(n_probes * rows, latents), u_full], 0)
        flowed, logdet = series(n, t, n_probes, w_in, out_weight, lhs, u_slice)
        return flowed, logdet[:, 0]

    return local


def solution(mesh):
    in_specs = (
        P("dp", None),
        P(None, "tensor"),
        P("tensor", None),
        P("dp", "tensor"),
        P("dp", "tensor"),
        P("dp", "tensor"),
        P(None, "dp", None),
    )
    out_specs = (P("dp", "tensor"), P("dp"))
    local = make_local(mesh.shape["dp"], mesh.shape["tensor"])
    return jax.shard_map(local, mesh=mesh, in_specs=in_specs, out_specs=out_specs, check_vma=False)
```

time: 454 us -> 400 us (0.88)
  waiting for transfers between devices: 205 us -> 120 us
  Pallas kernels: 178 us -> 244 us
  matrix products: 35.7 us -> 5.78 us
    ppermute x2 -> x1, waiting for transfers between devices: 180 us -> 79.5 us  [gather_blocks(): lax.ppermute(shard, 'dp', [((y + k) % half * 2 + c, y * 2 + c) for y in r...]
    pallas_call x1, Pallas kernels: 178 us -> 244 us  [series(): pl.pallas_call(functools.partial(series_kernel, n, nt, nx, n_probes), out...]
    dot_general x9 -> x1, matrix products: 35.7 us -> 5.78 us  [dot(): return jnp.dot(a, b, preferred_element_type=jnp.float32)]
    all_gather x1, waiting for transfers between devices: 24.8 us -> 40.8 us  [local(): u_full = lax.all_gather(u_slice, 'tensor', axis=1, tiled=True)]
  transfers between devices with their start and end apart: 8 -> 5, of which waited for: 3 -> 2; matrix products, arithmetic and copies ran while one was open for 7% -> 4% of each run, Pallas kernels for 0% -> 0%
where the time goes in v3:
time: 400 us
  Pallas kernels  244 us (61%)
  waiting for transfers between devices  120 us (30%)
  between operations  14.1 us (4%)
  local copies, waits for them, and re-layouts  9.76 us (2%)
  matrix products  5.78 us (1%)
  other arithmetic  4.95 us (1%)
    pallas_call x1, Pallas kernels, series(): pl.pallas_call(functools.partial(series_kernel, n, nt, nx, n_probes), out...  244 us
    ppermute x1, waiting for transfers between devices, gather_blocks(): lax.ppermute(shard, 'dp', [((y + k) % half * 2 + c, y * 2 + c) for y in r...  79.5 us
    all_gather x1, waiting for transfers between devices, local(): u_full = lax.all_gather(u_slice, 'tensor', axis=1, tiled=True)  40.8 us
  transfers between devices with their start and end apart: 5, of which 2 were waited for; matrix products, arithmetic and copies ran while one was open for 4% of the time, Pallas kernels for 0%

profile of v3, /device:TPU:6, one launch (start us, length us, event | category | flops | bytes accessed | tf_op | source)
XLA Modules:
  0.0 399.6 jit_solution(12076494189195481816)
XLA Ops:
  7.2 0.0 copy-start
  7.2 0.0 reduce-scatter.2.cloned.1.call-start
  7.2 0.6 collective-permute-start.1
  7.8 0.6 copy-done
  8.4 5.8 %convolution_convert_fusion = bf16[128,8192]{1,0:T(8,128)(2,1)} fusion(bf16[256,8192]{1,0:T(8,128)(2,1)} %param.9, bf16[128,4096]{1,0:T(8,128)(2,1)S(1)} %copy-done, bf16[4096,256]{1,0:T(8,128)(2,1)} %param.8), kind=kOutput, calls=%fused_computation | convolution fusion | flops 806518784 | bytes 9437184 | tf_op jit(solution)/shard_map/dot_general | solution.py:12
  14.2 3.2 copy.9
  17.4 0.0 copy-start.2
  17.4 2.8 copy.10
  20.2 0.0 copy-start.1
  20.2 0.0 reduce-scatter.2.cloned.1.call-update
  20.2 0.0 all-gather.2.cloned.1.call-start
  20.3 0.1 collective-permute-start
  20.4 79.5 %collective-permute-done.1.refs_2_ = bf16[1024,2048]{1,0:T(8,128)(2,1)} collective-permute-done((bf16[1024,2048]{1,0:T(8,128)(2,1)}, bf16[1024,2048]{1,0:T(8,128)(2,1)}, u32[]{:S(2)}, u32[]{:S(2)}) %collective-permute-start.1) | collective-permute-done | bytes 4194336 | tf_op jit(solution)/shard_map/ppermute | solution.py:26
  99.9 0.0 collective-permute-start.2
  99.9 0.0 reduce-scatter.2.cloned.1.call-done
  99.9 1.0 convert_element_type.17
  100.9 0.0 copy-done.2
  100.9 0.8 fusion.2.refs_6_
  101.8 0.0 all-gather.2.cloned.1.call-update
  101.8 40.8 %all-gather.2.cloned.1.call-done = bf16[128,4096]{1,0:T(8,128)(2,1)} async-done(((bf16[128,512]{1,0:T(8,128)(2,1)}), bf16[128,4096]{1,0:T(8,128)(2,1)}) %all-gather.2.cloned.1.call-update) | async-done | bytes 1048592 | tf_op jit(solution)/shard_map/all_gather | solution.py:464
  142.6 0.0 copy-done.1
  142.6 3.1 pad_maximum_fusion.refs_5_
  145.7 0.0 collective-permute-done.refs_1_
  145.7 0.0 collective-permute-done.2.refs_3_
  145.7 243.9 %shard_map.86 = (f32[128,512]{1,0:T(8,128)}, f32[128,128]{1,0:T(8,128)}) custom-call(bf16[1024,2048]{1,0:T(8,128)(2,1)} %refs_0_.1, bf16[1024,2048]{1,0:T(8,128)(2,1)} %collective-permute-done.refs_1_, bf16[1024,2048]{1,0:T(8,128)(2,1)} %collective-permute-done.1.refs_2_, bf16[1024,2048]{1,0:T(8,128)(2,1)} %collective-permute-done.2.refs_3_, ...), custom_call_target="tpu_custom_call" | custom-call | flops 25769803776 | bytes 33554432 | tf_op jit(solution)/shard_map/pallas_call | solution.py:407
  389.6 1.5 slice_reduce_fusion
  391.1 1.7 copy.12
Async XLA Ops:
  7.2 1.2 copy-start
  7.2 92.7 %reduce-scatter.2.cloned.1.call-start = ((), (), s32[]{:S(2)}) async-start(), calls=%async_computation.1 | async-start | bytes 2359296 | tf_op jit(solution)/shard_map/reduce_scatter | solution.py:457
  7.2 92.7 %collective-permute-start.1 = (bf16[1024,2048]{1,0:T(8,128)(2,1)}, bf16[1024,2048]{1,0:T(8,128)(2,1)}, u32[]{:S(2)}, u32[]{:S(2)}) collective-permute-start(bf16[1024,2048]{1,0:T(8,128)(2,1)} %refs_0_.1), channel_id=1, source_target_pairs={{16,0},{24,8},{0,16},{8,24},{17,1},{25,9},{1,17},{9,25},{18,2},{26... | collective-permute-start | bytes 12582920 | tf_op jit(solution)/shard_map/ppermute | solution.py:26
  17.4 83.5 %copy-start.2 = (bf16[128,512]{1,0:T(8,128)(2,1)S(1)}, bf16[128,512]{1,0:T(8,128)(2,1)}, u32[]{:S(2)}) copy-start(bf16[128,512]{1,0:T(8,128)(2,1)} %param.10) | copy-start | bytes 393220
  20.2 122.4 %copy-start.1 = (bf16[2,128,4096]{2,1,0:T(8,128)(2,1)S(1)}, bf16[2,128,4096]{2,1,0:T(8,128)(2,1)}, u32[]{:S(2)}) copy-start(bf16[2,128,4096]{2,1,0:T(8,128)(2,1)} %param.13) | copy-start | bytes 6291460
  20.2 122.3 %all-gather.2.cloned.1.call-start = ((), (), s32[]{:S(2)}) async-start(), calls=%async_computation.2 | async-start | bytes 1179648 | tf_op jit(solution)/shard_map/all_gather | solution.py:464
  20.3 125.4 %collective-permute-start = (bf16[1024,2048]{1,0:T(8,128)(2,1)}, bf16[1024,2048]{1,0:T(8,128)(2,1)}, u32[]{:S(2)}, u32[]{:S(2)}) collective-permute-start(bf16[1024,2048]{1,0:T(8,128)(2,1)} %refs_0_.1), channel_id=1, source_target_pairs={{0,8},{8,0},{16,24},{24,16},{1,9},{9,1},{17,25},{25,17},{2,10},{10... | collective-permute-start | bytes 12582920 | tf_op jit(solution)/shard_map/ppermute | solution.py:29
  99.9 45.8 %collective-permute-start.2 = (bf16[1024,2048]{1,0:T(8,128)(2,1)}, bf16[1024,2048]{1,0:T(8,128)(2,1)}, u32[]{:S(2)}, u32[]{:S(2)}) collective-permute-start(bf16[1024,2048]{1,0:T(8,128)(2,1)} %collective-permute-done.1.refs_2_), channel_id=1, source_target_pairs={{0,8},{8,0},{16,24},{24,16},{1,9},{9,1},{17,25},{25,17},{2,10},{10... | collective-permute-start | bytes 12582920 | tf_op jit(solution)/shard_map/ppermute | solution.py:29
Sparse Core Ops, SparseCore 0:
  20.4 68.5 reduce-scatter.1
  101.9 40.5 all-gather.1

commit v4 on v3

--- a/solution.py
+++ b/solution.py
@@ -46,7 +46,7 @@
     w_in = refs[:n]
     w_shard, lhs, u_ref, flowed_ref, log_ref = refs[n : n + 5]
     (win, wout, sr, mix, slope, full, sendx, xbuf, own, zbuf, left, right, pbuf, pxbuf, pzbuf,
-     in_sem, out_sem, ys, yr, fs, fr, cs, cr,
+     ubuf, in_sem, out_sem, ys, yr, fs, fr, cs, cr, us, ur, vs, vr,
      xs, xr, zs, zr, gs, gr, hs, hr, pxs, pxr, pzs, pzr) = refs[n + 5 :]
     nz = nt // nx
     half = n // 2
@@ -123,20 +123,56 @@
     load_out.start()
     ccopy(me).start()
 
-    for b in range(n):
-        loads_in[b].wait()
-
-        def first_pass(i, _):
-            value = dot(lhs[:, block(held[b])], win[block(held[b]), at(i)])
-            left[:, at(i)] = value[:big] if b == 0 else left[:, at(i)] + value[:big]
-            slope[:, at(i)] = value[big:] if b == 0 else slope[:, at(i)] + value[big:]
-            return 0
-
-        lax.fori_loop(0, tiles, first_pass, 0)
-        if b == n // 2:
-            for k in range(1, half):
-                for p in range(1, pieces):
-                    ycopy(k, p).start()
+    def slot(k, j):
+        return lax.rem(z + nz - k, nz) * nx + lax.rem(x + nx - j, nx)
+
+    def ucopy(k):
+        return remote(ubuf.at[t], ubuf.at[t], us.at[k - 1], ur.at[k - 1], dev(zup(k), x))
+
+    def uarrive(k):
+        part = ubuf.at[slot(k, 0)]
+        return remote(part, part, us.at[k - 1], ur.at[k - 1], dev(zup(k), x))
+
+    def vcopy(k, j):
+        part = ubuf.at[slot(k, 0)]
+        return remote(part, part, vs.at[k, j - 1], vr.at[k, j - 1], dev(z, xup(j)))
+
+    def varrive(k, j):
+        part = ubuf.at[slot(k, j)]
+        return remote(part, part, vs.at[k, j - 1], vr.at[k, j - 1], dev(z, xup(j)))
+
+    ubuf[t] = u_ref[...]
+    for k in range(1, nz):
+        ucopy(k).start()
+    for j in range(1, nx):
+        vcopy(0, j).start()
+
+    for c in loads_in:
+        c.wait()
+
+    def first_pass(i, _):
+        left[:, at(i)] = dot(lhs[...], win[:, at(i)])
+        return 0
+
+    lax.fori_loop(0, tiles, first_pass, 0)
+    for k in range(1, half):
+        for p in range(1, pieces):
+            ycopy(k, p).start()
+    for k in range(1, nz):
+        uarrive(k).wait_recv()
+        for j in range(1, nx):
+            vcopy(k, j).start()
+    for k in range(nz):
+        for j in range(1, nx):
+            varrive(k, j).wait_recv()
+
+    def second_pass(i, _):
+        slope[:, at(i)] = sum(
+            dot(ubuf[c], win[pl.ds(c * chunk, chunk), at(i)]) for c in range(nt)
+        )
+        return 0
+
+    lax.fori_loop(0, tiles, second_pass, 0)
 
     def activate(i, _):
         th = jnp.tanh(slope[:, at(i)])
@@ -225,12 +261,46 @@
         a, b = held[2 * k], held[2 * k + 1]
         return [a, b] if n == nz else [lax.div(a, n // nz)]
 
+    def gcopy(kind, k):
+        part = full.at[t, gbands[kind]]
+        return remote(part, part, gs.at[kind, k - 1], gr.at[kind, k - 1], dev(zup(k), x))
+
+    def garrive(kind, k):
+        part = full.at[slot(k, 0), gbands[kind]]
+        return remote(part, part, gs.at[kind, k - 1], gr.at[kind, k - 1], dev(zup(k), x))
+
+    def hcopy(kind, k, j):
+        part = full.at[slot(k, 0), gbands[kind]]
+        return remote(part, part, hs.at[kind, k, j - 1], hr.at[kind, k, j - 1], dev(z, xup(j)))
+
+    def harrive(kind, k, j):
+        part = full.at[slot(k, j), gbands[kind]]
+        return remote(part, part, hs.at[kind, k, j - 1], hr.at[kind, k, j - 1], dev(z, xup(j)))
+
+    def send_own(kind):
+        for k in range(1, nz):
+            gcopy(kind, k).start()
+        for j in range(1, nx):
+            hcopy(kind, 0, j).start()
+
+    early = jnp.bool_(False)
+    if pieces > 1:
+        for k in range(half - 1):
+            for zt in group_rows(k):
+                early = jnp.logical_or(early, z == zt)
+
+    def finish_rows():
+        summed(M)
+        send_own(M)
+
     load_out.wait()
     whole_block(me)
     ccopy(held[1]).wait_recv()
     whole_block(held[1])
     for k in range(1, half):
         for p in range(pieces):
+            if k == half - 1 and p and p == pieces - 1:
+                pl.when(early)(finish_rows)
             yarrive(k, p).wait_recv()
             fcopy(k, p).start()
             if p == 0:
@@ -276,25 +346,6 @@
 
     lax.fori_loop(0, nz, scatter, 0)
 
-    def gcopy(kind, k):
-        part = full.at[t, gbands[kind]]
-        return remote(part, part, gs.at[kind, k - 1], gr.at[kind, k - 1], dev(zup(k), x))
-
-    def slot(k, j):
-        return lax.rem(z + nz - k, nz) * nx + lax.rem(x + nx - j, nx)
-
-    def garrive(kind, k):
-        part = full.at[slot(k, 0), gbands[kind]]
-        return remote(part, part, gs.at[kind, k - 1], gr.at[kind, k - 1], dev(zup(k), x))
-
-    def hcopy(kind, k, j):
-        part = full.at[slot(k, 0), gbands[kind]]
-        return remote(part, part, hs.at[kind, k, j - 1], hr.at[kind, k, j - 1], dev(z, xup(j)))
-
-    def harrive(kind, k, j):
-        part = full.at[slot(k, j), gbands[kind]]
-        return remote(part, part, hs.at[kind, k, j - 1], hr.at[kind, k, j - 1], dev(z, xup(j)))
-
     def consume(kind, c):
         off = pl.ds(pl.multiple_of(c * chunk, chunk), chunk)
         acc, weight = (left, win) if kind == M else (right, wout)
@@ -305,14 +356,7 @@
 
         lax.fori_loop(0, tiles, body, 0)
 
-    def send_own(kind):
-        for k in range(1, nz):
-            gcopy(kind, k).start()
-        for j in range(1, nx):
-            hcopy(kind, 0, j).start()
-
-    summed(M)
-    send_own(M)
+    pl.when(jnp.logical_not(early))(finish_rows)
     finish(W, z)
     consume(M, t)
     summed(W)
@@ -384,6 +428,11 @@
         pzcopy(k).wait_send()
     for j in range(1, nx):
         pxcopy(j).wait_send()
+    for k in range(nz):
+        for j in range(1, nx):
+            vcopy(k, j).wait_send()
+    for k in range(1, nz):
+        ucopy(k).wait_send()
     ccopy(me).wait_send()
     for k in range(1, half):
         for p in range(pieces):
@@ -425,10 +474,13 @@
             pltpu.VMEM((2, rows, 128), f32),
             pltpu.VMEM((nx - 1, rows, 128), f32),
             pltpu.VMEM((nz - 1, rows, 128), f32),
+            pltpu.VMEM((nt, rows, chunk), bf),
             dma((n,)), dma,
             dma((half - 1, pieces)), dma((half - 1, pieces)),
             dma((half - 1, pieces)), dma((half - 1, pieces)),
             dma, dma,
+            dma((nz - 1,)), dma((nz - 1,)),
+            dma((nz, nx - 1)), dma((nz, nx - 1)),
             dma((2, nz, nx - 1)), dma((2, nz, nx - 1)),
             dma((2, nz - 1)), dma((2, nz - 1)),
             dma((2, nz - 1)), dma((2, nz - 1)),
@@ -461,9 +513,7 @@
         u_slice = (
             moments[:, 0] + jax.nn.softplus(moments[:, 1]) * noise.astype(jnp.float32)
         ).astype(jnp.bfloat16)
-        u_full = lax.all_gather(u_slice, "tensor", axis=1, tiled=True)
-
-        lhs = jnp.concatenate([probes.reshape(n_probes * rows, latents), u_full], 0)
+        lhs = probes.reshape(n_probes * rows, latents)
         flowed, logdet = series(n, t, n_probes, w_in, out_weight, lhs, u_slice)
         return flowed, logdet[:, 0]
 

time: 400 us -> 354 us (0.89)
  waiting for transfers between devices: 120 us -> 85.3 us
  Pallas kernels: 244 us -> 235 us
    all_gather x1 -> x0, waiting for transfers between devices: 40.8 us -> none  [local(): u_full = lax.all_gather(u_slice, 'tensor', axis=1, tiled=True)]
    pallas_call x1, Pallas kernels: 244 us -> 235 us  [series(): pl.pallas_call(functools.partial(series_kernel, n, nt, nx, n_probes), out...]
    ppermute x2, waiting for transfers between devices: 0.01 us -> 5.64 us  [gather_blocks(): blocks += [own, lax.ppermute(own, 'dp', swap)]]
  transfers between devices with their start and end apart: 5 -> 4, of which waited for: 2 -> 2; matrix products, arithmetic and copies ran while one was open for 4% -> 4% of each run, Pallas kernels for 0% -> 0%
where the time goes in v4:
time: 354 us; the launch traced here: 352 us
  Pallas kernels  235 us (66%)
  waiting for transfers between devices  85.3 us (24%)
  between operations  14.1 us (4%)
  local copies, waits for them, and re-layouts  9.77 us (3%)
  matrix products  5.77 us (2%)
    pallas_call x1, Pallas kernels, series(): pl.pallas_call(functools.partial(series_kernel, n, nt, nx, n_probes), out...  235 us
    ppermute x1, waiting for transfers between devices, gather_blocks(): lax.ppermute(shard, 'dp', [((y + k) % half * 2 + c, y * 2 + c) for y in r...  79.6 us
  transfers between devices with their start and end apart: 4, of which 2 were waited for; matrix products, arithmetic and copies ran while one was open for 4% of the time, Pallas kernels for 0%

profile of v4, /device:TPU:6, one launch (start us, length us, event | category | flops | bytes accessed | tf_op | source)
XLA Modules:
  0.0 352.1 jit_solution(4408517388344000344)
XLA Ops:
  7.2 0.0 copy-start
  7.2 0.0 reduce-scatter.2.cloned.1.call-start
  7.2 0.6 collective-permute-start.1
  7.8 0.6 copy-done
  8.4 5.8 %convolution_convert_fusion = bf16[128,8192]{1,0:T(8,128)(2,1)} fusion(bf16[256,8192]{1,0:T(8,128)(2,1)} %param.9, bf16[128,4096]{1,0:T(8,128)(2,1)S(1)} %copy-done, bf16[4096,256]{1,0:T(8,128)(2,1)} %param.8), kind=kOutput, calls=%fused_computation | convolution fusion | flops 806518784 | bytes 9437184 | tf_op jit(solution)/shard_map/dot_general | solution.py:12
  14.2 3.2 copy.9
  17.4 0.0 copy-start.1
  17.4 2.8 copy.10
  20.2 0.0 reduce-scatter.2.cloned.1.call-update
  20.2 0.1 collective-permute-start
  20.3 79.6 %collective-permute-done.1.refs_2_ = bf16[1024,2048]{1,0:T(8,128)(2,1)} collective-permute-done((bf16[1024,2048]{1,0:T(8,128)(2,1)}, bf16[1024,2048]{1,0:T(8,128)(2,1)}, u32[]{:S(2)}, u32[]{:S(2)}) %collective-permute-start.1) | collective-permute-done | bytes 4194336 | tf_op jit(solution)/shard_map/ppermute | solution.py:26
  99.9 0.0 collective-permute-start.2
  99.9 0.0 reduce-scatter.2.cloned.1.call-done
  99.9 1.0 convert_element_type.17
  100.9 0.0 copy-done.1
  100.9 0.8 fusion.2.refs_6_
  101.8 0.0 collective-permute-done.refs_1_
  101.8 5.6 %collective-permute-done.2.refs_3_ = bf16[1024,2048]{1,0:T(8,128)(2,1)} collective-permute-done((bf16[1024,2048]{1,0:T(8,128)(2,1)}, bf16[1024,2048]{1,0:T(8,128)(2,1)}, u32[]{:S(2)}, u32[]{:S(2)}) %collective-permute-start.2) | collective-permute-done | bytes 4194336 | tf_op jit(solution)/shard_map/ppermute | solution.py:29
  107.4 234.7 %shard_map.86 = (f32[128,512]{1,0:T(8,128)}, f32[128,128]{1,0:T(8,128)}) custom-call(bf16[1024,2048]{1,0:T(8,128)(2,1)} %refs_0_.1, bf16[1024,2048]{1,0:T(8,128)(2,1)} %collective-permute-done.refs_1_, bf16[1024,2048]{1,0:T(8,128)(2,1)} %collective-permute-done.1.refs_2_, bf16[1024,2048]{1,0:T(8,128)(2,1)} %collective-permute-done.2.refs_3_, ...), custom_call_target="tpu_custom_call" | custom-call | flops 25769803776 | bytes 33554432 | tf_op jit(solution)/shard_map/pallas_call | solution.py:456
  342.1 1.5 slice_reduce_fusion
  343.6 1.7 copy.12
Async XLA Ops:
  7.2 1.2 copy-start
  7.2 92.7 %reduce-scatter.2.cloned.1.call-start = ((), (), s32[]{:S(2)}) async-start(), calls=%async_computation.1 | async-start | bytes 2359296 | tf_op jit(solution)/shard_map/reduce_scatter | solution.py:509
  7.2 92.7 %collective-permute-start.1 = (bf16[1024,2048]{1,0:T(8,128)(2,1)}, bf16[1024,2048]{1,0:T(8,128)(2,1)}, u32[]{:S(2)}, u32[]{:S(2)}) collective-permute-start(bf16[1024,2048]{1,0:T(8,128)(2,1)} %refs_0_.1), channel_id=1, source_target_pairs={{16,0},{24,8},{0,16},{8,24},{17,1},{25,9},{1,17},{9,25},{18,2},{26... | collective-permute-start | bytes 12582920 | tf_op jit(solution)/shard_map/ppermute | solution.py:26
  17.4 83.5 %copy-start.1 = (bf16[128,512]{1,0:T(8,128)(2,1)S(1)}, bf16[128,512]{1,0:T(8,128)(2,1)}, u32[]{:S(2)}) copy-start(bf16[128,512]{1,0:T(8,128)(2,1)} %param.10) | copy-start | bytes 393220
  20.2 81.5 %collective-permute-start = (bf16[1024,2048]{1,0:T(8,128)(2,1)}, bf16[1024,2048]{1,0:T(8,128)(2,1)}, u32[]{:S(2)}, u32[]{:S(2)}) collective-permute-start(bf16[1024,2048]{1,0:T(8,128)(2,1)} %refs_0_.1), channel_id=1, source_target_pairs={{0,8},{8,0},{16,24},{24,16},{1,9},{9,1},{17,25},{25,17},{2,10},{10... | collective-permute-start | bytes 12582920 | tf_op jit(solution)/shard_map/ppermute | solution.py:29
  99.9 7.5 %collective-permute-start.2 = (bf16[1024,2048]{1,0:T(8,128)(2,1)}, bf16[1024,2048]{1,0:T(8,128)(2,1)}, u32[]{:S(2)}, u32[]{:S(2)}) collective-permute-start(bf16[1024,2048]{1,0:T(8,128)(2,1)} %collective-permute-done.1.refs_2_), channel_id=1, source_target_pairs={{0,8},{8,0},{16,24},{24,16},{1,9},{9,1},{17,25},{25,17},{2,10},{10... | collective-permute-start | bytes 12582920 | tf_op jit(solution)/shard_map/ppermute | solution.py:29
Sparse Core Ops, SparseCore 0:
  20.4 68.5 reduce-scatter.1

commit v5 on v4

--- a/solution.py
+++ b/solution.py
@@ -283,11 +283,45 @@
         for j in range(1, nx):
             hcopy(kind, 0, j).start()
 
-    early = jnp.bool_(False)
-    if pieces > 1:
+    def consume(kind, c):
+        off = pl.ds(pl.multiple_of(c * chunk, chunk), chunk)
+        acc, weight = (left, win) if kind == M else (right, wout)
+
+        def body(i, _):
+            acc[:, at(i)] += dot(full[c, gbands[kind], :], weight[off, at(i)])
+            return 0
+
+        lax.fori_loop(0, tiles, body, 0)
+
+    def is_early(zz):
+        found = jnp.bool_(False)
         for k in range(half - 1):
             for zt in group_rows(k):
-                early = jnp.logical_or(early, z == zt)
+                found = jnp.logical_or(found, zz == zt)
+        return found
+
+    def row(k):
+        return lax.rem(z + nz - k, nz)
+
+    early = is_early(z)
+
+    def forward(kind, k):
+        garrive(kind, k).wait_recv()
+        for j in range(1, nx):
+            hcopy(kind, k, j).start()
+        consume(kind, slot(k, 0))
+
+    def take(kind, k):
+        for j in range(1, nx):
+            harrive(kind, k, j).wait_recv()
+            consume(kind, slot(k, j))
+
+    def early_rows():
+        pl.when(early)(lambda: consume(M, t))
+        for k in range(1, nz):
+            pl.when(is_early(row(k)))(functools.partial(forward, M, k))
+        for k in range(nz):
+            pl.when(is_early(row(k)))(functools.partial(take, M, k))
 
     def finish_rows():
         summed(M)
@@ -299,13 +333,15 @@
     whole_block(held[1])
     for k in range(1, half):
         for p in range(pieces):
-            if k == half - 1 and p and p == pieces - 1:
-                pl.when(early)(finish_rows)
-            yarrive(k, p).wait_recv()
-            fcopy(k, p).start()
             if p == 0:
                 for zt in group_rows(k - 1):
                     finish(M, zt)
+                if k == half - 1:
+                    pl.when(early)(finish_rows)
+            if k == half - 1 and p == pieces - 1:
+                early_rows()
+            yarrive(k, p).wait_recv()
+            fcopy(k, p).start()
             process(held[2 * k], p)
             fcopy(k, p, False).wait_recv()
             process(held[2 * k + 1], p)
@@ -346,19 +382,9 @@
 
     lax.fori_loop(0, nz, scatter, 0)
 
-    def consume(kind, c):
-        off = pl.ds(pl.multiple_of(c * chunk, chunk), chunk)
-        acc, weight = (left, win) if kind == M else (right, wout)
-
-        def body(i, _):
-            acc[:, at(i)] += dot(full[c, gbands[kind], :], weight[off, at(i)])
-            return 0
-
-        lax.fori_loop(0, tiles, body, 0)
-
     pl.when(jnp.logical_not(early))(finish_rows)
     finish(W, z)
-    consume(M, t)
+    pl.when(jnp.logical_not(early))(lambda: consume(M, t))
     summed(W)
     send_own(W)
     for p in range(n_probes):
@@ -368,22 +394,15 @@
     consume(W, t)
 
     def gather(k, _):
-        for kind in (M, W):
-            garrive(kind, k).wait_recv()
-            for j in range(1, nx):
-                hcopy(kind, k, j).start()
-            consume(kind, slot(k, 0))
-        for kind in (M, W):
-            for j in range(1, nx):
-                harrive(kind, k - 1, j).wait_recv()
-                consume(kind, slot(k - 1, j))
+        pl.when(jnp.logical_not(is_early(row(k))))(lambda: forward(M, k))
+        forward(W, k)
+        pl.when(jnp.logical_not(is_early(row(k - 1))))(lambda: take(M, k - 1))
+        take(W, k - 1)
         return 0
 
     lax.fori_loop(1, nz, gather, 0)
-    for kind in (M, W):
-        for j in range(1, nx):
-            harrive(kind, nz - 1, j).wait_recv()
-            consume(kind, slot(nz - 1, j))
+    pl.when(jnp.logical_not(is_early(row(nz - 1))))(lambda: take(M, nz - 1))
+    take(W, nz - 1)
 
     total = jnp.zeros((rows, 1), jnp.float32)
     for p in range(n_probes):

time: 354 us -> 358 us (1.011)
  Pallas kernels: 235 us -> 240 us
    pallas_call x1, Pallas kernels: 235 us -> 240 us  [series(): pl.pallas_call(functools.partial(series_kernel, n, nt, nx, n_probes), out...]
where the time goes in v5:
time: 358 us
  Pallas kernels  240 us (67%)
  waiting for transfers between devices  85.3 us (24%)
  between operations  14.1 us (4%)
  local copies, waits for them, and re-layouts  9.77 us (3%)
  matrix products  5.77 us (2%)
    pallas_call x1, Pallas kernels, series(): pl.pallas_call(functools.partial(series_kernel, n, nt, nx, n_probes), out...  240 us
    ppermute x1, waiting for transfers between devices, gather_blocks(): lax.ppermute(shard, 'dp', [((y + k) % half * 2 + c, y * 2 + c) for y in r...  79.6 us
  transfers between devices with their start and end apart: 4, of which 2 were waited for; matrix products, arithmetic and copies ran while one was open for 4% of the time, Pallas kernels for 0%

profile of v5, /device:TPU:6, one launch (start us, length us, event | category | flops | bytes accessed | tf_op | source)
XLA Modules:
  0.0 357.7 jit_solution(2586993422333443522)
XLA Ops:
  7.2 0.0 copy-start
  7.2 0.0 reduce-scatter.2.cloned.1.call-start
  7.2 0.6 collective-permute-start.1
  7.8 0.6 copy-done
  8.4 5.8 %convolution_convert_fusion = bf16[128,8192]{1,0:T(8,128)(2,1)} fusion(bf16[256,8192]{1,0:T(8,128)(2,1)} %param.9, bf16[128,4096]{1,0:T(8,128)(2,1)S(1)} %copy-done, bf16[4096,256]{1,0:T(8,128)(2,1)} %param.8), kind=kOutput, calls=%fused_computation | convolution fusion | flops 806518784 | bytes 9437184 | tf_op jit(solution)/shard_map/dot_general | solution.py:12
  14.2 3.2 copy.9
  17.4 0.0 copy-start.1
  17.4 2.8 copy.10
  20.2 0.0 reduce-scatter.2.cloned.1.call-update
  20.2 0.1 collective-permute-start
  20.3 79.6 %collective-permute-done.1.refs_2_ = bf16[1024,2048]{1,0:T(8,128)(2,1)} collective-permute-done((bf16[1024,2048]{1,0:T(8,128)(2,1)}, bf16[1024,2048]{1,0:T(8,128)(2,1)}, u32[]{:S(2)}, u32[]{:S(2)}) %collective-permute-start.1) | collective-permute-done | bytes 4194336 | tf_op jit(solution)/shard_map/ppermute | solution.py:26
  99.9 0.0 collective-permute-start.2
  99.9 0.0 reduce-scatter.2.cloned.1.call-done
  99.9 1.0 convert_element_type.17
  100.9 0.0 copy-done.1
  100.9 0.8 fusion.2.refs_6_
  101.8 0.0 collective-permute-done.refs_1_
  101.8 5.6 %collective-permute-done.2.refs_3_ = bf16[1024,2048]{1,0:T(8,128)(2,1)} collective-permute-done((bf16[1024,2048]{1,0:T(8,128)(2,1)}, bf16[1024,2048]{1,0:T(8,128)(2,1)}, u32[]{:S(2)}, u32[]{:S(2)}) %collective-permute-start.2) | collective-permute-done | bytes 4194336 | tf_op jit(solution)/shard_map/ppermute | solution.py:29
  107.4 240.3 %shard_map.86 = (f32[128,512]{1,0:T(8,128)}, f32[128,128]{1,0:T(8,128)}) custom-call(bf16[1024,2048]{1,0:T(8,128)(2,1)} %refs_0_.1, bf16[1024,2048]{1,0:T(8,128)(2,1)} %collective-permute-done.refs_1_, bf16[1024,2048]{1,0:T(8,128)(2,1)} %collective-permute-done.1.refs_2_, bf16[1024,2048]{1,0:T(8,128)(2,1)} %collective-permute-done.2.refs_3_, ...), custom_call_target="tpu_custom_call" | custom-call | flops 25769803776 | bytes 33554432 | tf_op jit(solution)/shard_map/pallas_call | solution.py:475
  347.8 1.5 slice_reduce_fusion
  349.2 1.7 copy.12
Async XLA Ops:
  7.2 1.2 copy-start
  7.2 92.7 %reduce-scatter.2.cloned.1.call-start = ((), (), s32[]{:S(2)}) async-start(), calls=%async_computation.1 | async-start | bytes 2359296 | tf_op jit(solution)/shard_map/reduce_scatter | solution.py:528
  7.2 92.7 %collective-permute-start.1 = (bf16[1024,2048]{1,0:T(8,128)(2,1)}, bf16[1024,2048]{1,0:T(8,128)(2,1)}, u32[]{:S(2)}, u32[]{:S(2)}) collective-permute-start(bf16[1024,2048]{1,0:T(8,128)(2,1)} %refs_0_.1), channel_id=1, source_target_pairs={{16,0},{24,8},{0,16},{8,24},{17,1},{25,9},{1,17},{9,25},{18,2},{26... | collective-permute-start | bytes 12582920 | tf_op jit(solution)/shard_map/ppermute | solution.py:26
  17.4 83.5 %copy-start.1 = (bf16[128,512]{1,0:T(8,128)(2,1)S(1)}, bf16[128,512]{1,0:T(8,128)(2,1)}, u32[]{:S(2)}) copy-start(bf16[128,512]{1,0:T(8,128)(2,1)} %param.10) | copy-start | bytes 393220
  20.2 81.5 %collective-permute-start = (bf16[1024,2048]{1,0:T(8,128)(2,1)}, bf16[1024,2048]{1,0:T(8,128)(2,1)}, u32[]{:S(2)}, u32[]{:S(2)}) collective-permute-start(bf16[1024,2048]{1,0:T(8,128)(2,1)} %refs_0_.1), channel_id=1, source_target_pairs={{0,8},{8,0},{16,24},{24,16},{1,9},{9,1},{17,25},{25,17},{2,10},{10... | collective-permute-start | bytes 12582920 | tf_op jit(solution)/shard_map/ppermute | solution.py:29
  99.9 7.5 %collective-permute-start.2 = (bf16[1024,2048]{1,0:T(8,128)(2,1)}, bf16[1024,2048]{1,0:T(8,128)(2,1)}, u32[]{:S(2)}, u32[]{:S(2)}) collective-permute-start(bf16[1024,2048]{1,0:T(8,128)(2,1)} %collective-permute-done.1.refs_2_), channel_id=1, source_target_pairs={{0,8},{8,0},{16,24},{24,16},{1,9},{9,1},{17,25},{25,17},{2,10},{10... | collective-permute-start | bytes 12582920 | tf_op jit(solution)/shard_map/ppermute | solution.py:29
Sparse Core Ops, SparseCore 0:
  20.4 68.5 reduce-scatter.1
